TPU v7x, 32 devices: a whole 2x2x4 slice. The times are simulated.
32 devices in a mesh: seq: 8 (over z, x), mp: 4 (over y, core).
Axes of the slice: x: 2, y: 2, z: 4, core: 2. Of those that a mesh axis runs over, the one named last changes fastest.
Arguments:
- tokens: bfloat16 [4096, 4096], P('seq'), may hold values from -6 to 6
- w_query: bfloat16 [4096, 2048], P(None, 'mp'), may hold values from -0.09375 to 0.09375
- w_key: bfloat16 [4096, 2048], P(None, 'mp'), may hold values from -0.09375 to 0.09375
- w_value: bfloat16 [4096, 2048], P(None, 'mp'), may hold values from -0.09375 to 0.09375
- starts: int32 [6], replicated, may hold values from 1024 to 4095, as said below
- cotangent: bfloat16 [4096, 2048], P('seq', 'mp'), may hold values from -6 to 6
Outputs:
- attended: bfloat16 [4096, 2048], P('seq', 'mp')
- input_grad: bfloat16 [4096, 4096], P(('seq', 'mp'))
- grad_query: float32 [4096, 2048], P('seq', 'mp')
- grad_key: float32 [4096, 2048], P('seq', 'mp')
- grad_value: float32 [4096, 2048], P('seq', 'mp')
Inputs may be any that keep to these rules, and one draw needn't show every extreme that they name: The starts rise strictly; start number i (counting from 0) lies at or after 4096 // 4 + i * w and before 4096 // 4 + (i + 1) * w, with w = 512.
All inputs are finite; a program needn't handle non-finite values.
Results may differ from a plain program's by a relative error of at most 0.029.
Values may be sent and summed in bfloat16 or wider, within the bound.
A program may use at most 128 MiB of HBM per device.

v0:
```python
import functools

import jax
import jax.numpy as jnp
from jax import lax
from jax.experimental import pallas as pl
from jax.experimental.pallas import tpu as pltpu
from jax.sharding import PartitionSpec as P

DH = 128
F32 = jnp.float32
LOW = jnp.bfloat16


def params():
    return pltpu.CompilerParams(vmem_limit_bytes=48 * 1024 * 1024)


def cost(flops, bytes_accessed):
    return pl.CostEstimate(flops=flops, bytes_accessed=bytes_accessed, transcendentals=0)


def dot(a, b, contract):
    return lax.dot_general(a, b, (contract, ((), ())), preferred_element_type=F32)


def segments(starts_ref, count, begin, shape, dim):
    positions = begin + lax.broadcasted_iota(jnp.int32, shape, dim)
    ids = jnp.zeros(shape, jnp.int32)
    for i in range(count):
        ids = ids + (starts_ref[i] <= positions).astype(jnp.int32)
    return ids


def started(starts_ref, count, before):
    total = jnp.int32(0)
    for i in range(count):
        total = total + (starts_ref[i] < before).astype(jnp.int32)
    return total


def project_kernel(
    count, starts_ref, place_ref, x_ref, wq_ref, wk_ref, wv_ref, c_ref,
    q_ref, k_ref, v_ref, fwd_ref, bwd_ref, acc_ref,
):
    step = pl.program_id(0)
    x = x_ref[...]
    for i, w_ref in enumerate((wq_ref, wk_ref, wv_ref)):
        term = jnp.dot(x, w_ref[...], preferred_element_type=F32)

        @pl.when(step == 0)
        def _():
            acc_ref[i] = term

        @pl.when(step > 0)
        def _():
            acc_ref[i] += term

    @pl.when(step == pl.num_programs(0) - 1)
    def _():
        rows = x_ref.shape[0]
        begin = place_ref[0]
        seg = segments(starts_ref, count, begin, (rows, DH), 0)
        mask_in = seg == started(starts_ref, count, begin)
        mask_out = seg == started(starts_ref, count, begin + rows)
        for h in range(q_ref.shape[1] // DH):
            cols = slice(h * DH, (h + 1) * DH)
            q = acc_ref[0, :, cols].astype(LOW)
            k = acc_ref[1, :, cols].astype(LOW)
            v = acc_ref[2, :, cols].astype(LOW)
            q_ref[:, cols] = q
            k_ref[:, cols] = k
            v_ref[:, cols] = v
            kept = jnp.where(mask_out, k.astype(F32), 0.0).astype(LOW)
            fwd_ref[h] = (dot(kept, v, ((0,), (0,))) * (1.0 / DH)).astype(LOW)
            kept = jnp.where(mask_in, q.astype(F32), 0.0).astype(LOW)
            bwd_ref[h] = (dot(kept, c_ref[:, cols], ((0,), (0,))) * (1.0 / DH)).astype(LOW)


def project(starts, begin, tokens, weights, cotangent):
    rows, width = tokens.shape
    cols = weights[0].shape[1]
    heads = cols // DH
    depth = min(1024, width)
    whole = pl.BlockSpec((rows, cols), lambda i, *_: (0, 0))
    state = pl.BlockSpec((heads, DH, DH), lambda i, *_: (0, 0, 0))
    low = jax.ShapeDtypeStruct((rows, cols), LOW)
    part = jax.ShapeDtypeStruct((heads, DH, DH), LOW)
    return pl.pallas_call(
        functools.partial(project_kernel, starts.shape[0]),
        grid_spec=pltpu.PrefetchScalarGridSpec(
            num_scalar_prefetch=2,
            grid=(width // depth,),
            in_specs=[pl.BlockSpec((rows, depth), lambda i, *_: (0, i))]
            + [pl.BlockSpec((depth, cols), lambda i, *_: (i, 0))] * 3
            + [whole],
            out_specs=[whole] * 3 + [state] * 2,
            scratch_shapes=[pltpu.VMEM((3, rows, cols), F32)],
        ),
        out_shape=[low] * 3 + [part] * 2,
        compiler_params=params(),
        cost_estimate=cost(6 * rows * width * cols, 2 * (rows * width + 3 * width * cols)),
        name="project",
    )(starts, begin, tokens, *weights, cotangent)


def attend_kernel(
    count, starts_ref, place_ref, q_ref, k_ref, v_ref, c_ref, s_ref, r_ref,
    a_ref, dq_ref, dk_ref, dv_ref,
):
    rows = q_ref.shape[0]
    begin = place_ref[0]
    q, k, v, c = q_ref[...], k_ref[...], v_ref[...], c_ref[...]
    state, back = s_ref[0], r_ref[0]
    seg_t = segments(starts_ref, count, begin, (rows, 1), 0)
    seg_s = segments(starts_ref, count, begin, (1, rows), 1)
    at_t = lax.broadcasted_iota(jnp.int32, (rows, rows), 0)
    at_s = lax.broadcasted_iota(jnp.int32, (rows, rows), 1)
    pair = (seg_t == seg_s) & (at_t >= at_s)
    inner = (seg_t == started(starts_ref, count, begin)).astype(F32)
    outer = (seg_t == started(starts_ref, count, begin + rows)).astype(F32)
    scale = 1.0 / DH
    last = ((1,), (1,))
    scores = jnp.where(pair, dot(q, k, last) * scale, 0.0).astype(LOW)
    grads = jnp.where(pair, dot(c, v, last) * scale, 0.0).astype(LOW)
    plain, first = ((1,), (0,)), ((0,), (0,))
    a_ref[...] = (dot(scores, v, plain) + inner * dot(q, state, plain)).astype(LOW)
    dq_ref[...] = (dot(grads, k, plain) + inner * dot(c, state, last)).astype(LOW)
    dk_ref[...] = (dot(grads, q, first) + outer * dot(v, back, last)).astype(LOW)
    dv_ref[...] = (dot(scores, c, first) + outer * dot(k, back, plain)).astype(LOW)


def attend(starts, begin, queries, keys, values, cotangent, state_in, reverse_in):
    rows, cols = queries.shape
    heads = cols // DH
    block = pl.BlockSpec((rows, DH), lambda h, *_: (0, h))
    state = pl.BlockSpec((1, DH, DH), lambda h, *_: (h, 0, 0))
    return pl.pallas_call(
        functools.partial(attend_kernel, starts.shape[0]),
        grid_spec=pltpu.PrefetchScalarGridSpec(
            num_scalar_prefetch=2,
            grid=(heads,),
            in_specs=[block] * 4 + [state] * 2,
            out_specs=[block] * 4,
        ),
        out_shape=[jax.ShapeDtypeStruct((rows, cols), LOW)] * 4,
        compiler_params=params(),
        cost_estimate=cost(heads * 12 * rows * rows * DH, 16 * rows * cols),
        name="attend",
    )(starts, begin, queries, keys, values, cotangent, state_in, reverse_in)


def turn_kernel(list_ref, x_ref, o_ref):
    o_ref[...] = x_ref[...].T


def turn(blocks, tokens, piece):
    rows = tokens.shape[0]
    many = blocks.shape[0]
    return pl.pallas_call(
        turn_kernel,
        grid_spec=pltpu.PrefetchScalarGridSpec(
            num_scalar_prefetch=1,
            grid=(many,),
            in_specs=[pl.BlockSpec((rows, piece), lambda i, at: (0, at[i]))],
            out_specs=pl.BlockSpec((piece, rows), lambda i, at: (i, 0)),
        ),
        out_shape=jax.ShapeDtypeStruct((many * piece, rows), LOW),
        compiler_params=params(),
        cost_estimate=cost(0, 4 * many * piece * rows),
        name="turn",
    )(blocks, tokens)


def share_kernel(half, scale, order_ref, own_ref, near_ref, far_ref, g_ref, h_ref, o_ref):
    step = pl.program_id(0)
    total = jnp.dot(own_ref[...], g_ref[...], preferred_element_type=F32)

    def write(got):
        both = total + jnp.dot(got, h_ref[...], preferred_element_type=F32)
        o_ref[0] = (scale * both).astype(LOW)

    @pl.when(step < half)
    def _():
        write(near_ref[...])

    @pl.when(step >= half)
    def _():
        write(far_ref[...])


def share(order, own, near, far, grad_own, grad_got, scale):
    length = order.shape[0]
    piece = own.shape[0] // length
    rows, cols = grad_own.shape
    half = near.shape[0] // piece
    grad = pl.BlockSpec((rows, cols), lambda i, at: (0, 0))
    return pl.pallas_call(
        functools.partial(share_kernel, half, scale),
        grid_spec=pltpu.PrefetchScalarGridSpec(
            num_scalar_prefetch=1,
            grid=(length,),
            in_specs=[
                pl.BlockSpec((piece, rows), lambda i, at: (at[i], 0)),
                pl.BlockSpec((piece, rows), lambda i, at: (jnp.minimum(i, half - 1), 0)),
                pl.BlockSpec((piece, rows), lambda i, at: (jnp.maximum(i - half, 0), 0)),
                grad,
                grad,
            ],
            out_specs=pl.BlockSpec((1, piece, cols), lambda i, at: (at[i], 0, 0)),
        ),
        out_shape=jax.ShapeDtypeStruct((length, piece, cols), LOW),
        compiler_params=params(),
        cost_estimate=cost(
            4 * length * piece * rows * cols, 2 * (3 * length * piece * rows + 2 * rows * cols)
        ),
        name="share",
    )(order, own, near, far, grad_own, grad_got)


def inputs_kernel(q_ref, k_ref, v_ref, wq_ref, wk_ref, wv_ref, o_ref):
    last = ((1,), (1,))
    total = dot(q_ref[...], wq_ref[...], last)
    total = total + dot(k_ref[...], wk_ref[...], last)
    total = total + dot(v_ref[...], wv_ref[...], last)
    o_ref[...] = total.astype(LOW)


def inputs(grads, weights):
    rows, cols = grads[0].shape
    width = weights[0].shape[0]
    piece = min(512, width)
    return pl.pallas_call(
        inputs_kernel,
        grid=(width // piece,),
        in_specs=[pl.BlockSpec((rows, cols), lambda i: (0, 0))] * 3
        + [pl.BlockSpec((piece, cols), lambda i: (i, 0))] * 3,
        out_specs=pl.BlockSpec((rows, piece), lambda i: (0, i)),
        out_shape=jax.ShapeDtypeStruct((rows, width), LOW),
        compiler_params=params(),
        cost_estimate=cost(6 * rows * width * cols, 2 * (rows * width + 3 * width * cols)),
        name="inputs",
    )(*grads, *weights)


def linked_pairs(token_count, span_total, start_count):
    first = token_count // 4
    stratum = (token_count - first) // start_count
    size = token_count // span_total

    def possible(low, high):
        begin, end = (low + 1) * size, high * size
        return not any(
            begin <= first + i * stratum and first + (i + 1) * stratum <= end
            for i in range(start_count)
        )

    distances = {}
    for low in range(span_total):
        for high in range(low + 1, span_total):
            if possible(low, high):
                distances.setdefault(high - low, []).append((low, high))
    return distances


def linked_states(forward_part, backward_part, starts, row_count):
    span_total, span_index = lax.axis_size("seq"), lax.axis_index("seq")
    begin = span_index * row_count
    seg_before = jnp.sum((starts < begin).astype(jnp.int32))
    seg_last = jnp.sum((starts < begin + row_count).astype(jnp.int32))
    state_in = jnp.zeros(forward_part.shape, jnp.float32)
    reverse_in = jnp.zeros(backward_part.shape, jnp.float32)
    pairs_at = linked_pairs(row_count * span_total, span_total, starts.shape[0])
    for distance, pairs in pairs_at.items():
        got = lax.ppermute(forward_part, "seq", pairs)
        source_last = jnp.sum((starts < begin - (distance - 1) * row_count).astype(jnp.int32))
        state_in = state_in + jnp.where(source_last == seg_before, got.astype(jnp.float32), 0.0)
        got = lax.ppermute(backward_part, "seq", [(high, low) for low, high in pairs])
        source_before = jnp.sum((starts < begin + distance * row_count).astype(jnp.int32))
        reverse_in = reverse_in + jnp.where(source_before == seg_last, got.astype(jnp.float32), 0.0)
    return state_in.astype(jnp.bfloat16), reverse_in.astype(jnp.bfloat16)


def line_scatter(parts):
    span_total = lax.axis_size("seq")
    length = span_total // 2
    place = lax.axis_index("seq") // 2

    def part_for(target):
        return lax.dynamic_index_in_dim(parts, jnp.clip(target, 0, length - 1), 0, keepdims=False)

    total = part_for(place).astype(jnp.float32)
    for way in (1, -1):
        carried = None
        for step in range(1, length):
            ahead = way * (length - step)
            sent = part_for(place + ahead)
            if carried is not None:
                sent = (sent.astype(jnp.float32) + carried.astype(jnp.float32)).astype(jnp.bfloat16)
            pairs = [
                (s, s + 2 * way) for s in range(span_total) if 0 <= s // 2 + ahead < length
            ]
            carried = lax.ppermute(sent, "seq", pairs)
        if carried is not None:
            total = total + carried.astype(jnp.float32)
    return total


def halving_scatter(partial):
    count = lax.axis_size("mp")
    index = lax.axis_index("mp")
    size = partial.shape[0] // count

    def pick(k):
        return lax.dynamic_slice_in_dim(partial, jnp.bitwise_xor(index, k) * size, size, 0)

    held = {k: pick(k) for k in range(count)}
    bit = 1
    while bit < count:
        pairs = [(m, m ^ bit) for m in range(count)]
        away = [k for k in held if k & bit]
        sent = jnp.concatenate([held[k] for k in away], axis=0) if len(away) > 1 else held[away[0]]
        got = lax.ppermute(sent, "mp", pairs)
        kind = jnp.bfloat16
        held = {
            k ^ bit: (
                held[k ^ bit].astype(jnp.float32)
                + got[i * size : (i + 1) * size].astype(jnp.float32)
            ).astype(kind)
            for i, k in enumerate(away)
        }
        bit *= 2
    return held[0]


def on_device(tokens, w_query, w_key, w_value, starts, cotangent):
    row_count, width = tokens.shape
    span_total = lax.axis_size("seq")
    span_index = lax.axis_index("seq")
    side = span_index % 2
    length = span_total // 2
    half = length // 2
    piece = width // span_total
    grad_scale = float(row_count * span_total) ** (-0.5)
    swap = [(s, s ^ 1) for s in range(span_total)]
    mates = [(m, m ^ 1) for m in range(lax.axis_size("mp"))]
    begin = (span_index * row_count).astype(jnp.int32).reshape(1)
    weights = (w_query, w_key, w_value)

    turn_order = jnp.arange(length, dtype=jnp.int32)
    core = (lax.axis_index("mp") % 2).astype(jnp.int32)
    order = (turn_order + half * core) % length
    away = turn(2 * order[:half] + 1 - side, tokens, piece)
    begin, away = lax.optimization_barrier((begin, away))
    near = lax.ppermute(away, "seq", swap)
    far = lax.ppermute(near, "mp", mates)

    queries, keys, values, forward_part, backward_part = project(
        starts, begin, tokens, weights, cotangent
    )
    own = turn(2 * turn_order + side, tokens, piece)
    state_in, reverse_in = linked_states(forward_part, backward_part, starts, row_count)
    attended, *rows = attend(
        starts, begin, queries, keys, values, cotangent, state_in, reverse_in
    )
    got = [lax.ppermute(grad, "seq", swap) for grad in rows]
    shares = [
        share(order, own, near, far, mine, theirs, grad_scale) for mine, theirs in zip(rows, got)
    ]
    rows, shares[0] = lax.optimization_barrier((rows, shares[0]))
    sums = [line_scatter(parts) for parts in shares]
    input_grad = halving_scatter(inputs(rows, weights))
    return (attended, input_grad, *sums)


def solution(mesh):
    in_specs = (P("seq", None), P(None, "mp"), P(None, "mp"), P(None, "mp"), P(), P("seq", "mp"))
    out_specs = (
        P("seq", "mp"),
        P(("seq", "mp"), None),
        P("seq", "mp"),
        P("seq", "mp"),
        P("seq", "mp"),
    )
    return jax.shard_map(
        on_device, mesh=mesh, in_specs=in_specs, out_specs=out_specs, check_vma=False
    )
```

profile of v0, /device:TPU:17, one launch (start us, length us, event | category | flops | bytes accessed | tf_op | source)
XLA Modules:
  0.0 207.1 jit_solution(10977376959324062397)
XLA Ops:
  0.7 2.2 %copy-done = bf16[512,4096]{1,0:T(8,128)(2,1)S(1)} copy-done((bf16[512,4096]{1,0:T(8,128)(2,1)S(1)}, bf16[512,4096]{1,0:T(8,128)(2,1)}, u32[]{:S(2)}) %copy-start) | copy-done | bytes 4194328
  5.2 13.2 %project.1 = (bf16[512,512]{1,0:T(8,128)(2,1)S(1)}, bf16[512,512]{1,0:T(8,128)(2,1)S(1)}, bf16[512,512]{1,0:T(8,128)(2,1)S(1)}, bf16[4,128,128]{2,1,0:T(8,128)(2,1)S(1)}, bf16[4,128,128]{2,1,0:T(8,128)(2,1)S(1)}) custom-call(s32[6]{0:T(128)S(1)} %copy-done.8, s32[1]{0:T(128)} %bitcast.place_ref, bf16[512,4096]{1,0:T(8,128)(2,1)} %x_ref.5, ...), custom_call_target="tpu_custom_call" | custom-call | flops 6442450944 | bytes 16777216 | tf_op jit(solution)/shard_map/project/pallas_call | solution.py:89
  20.8 2.0 collective-permute-start.2
  23.6 3.2 %collective-permute-start = (bf16[4,128,128]{2,1,0:T(8,128)(2,1)S(1)}, bf16[4,128,128]{2,1,0:T(8,128)(2,1)S(1)}, u32[]{:S(2)}, u32[]{:S(2)}) collective-permute-start(bf16[4,128,128]{2,1,0:T(8,128)(2,1)S(1)} %get-tuple-element.24), channel_id=1, source_target_pairs={{0,4},{4,8},{8,12},{12,16},{16,20},{20,24},{24,28},{1,5},{5,9},{9,... | collective-permute-start | bytes 393224 | tf_op jit(solution)/shard_map/ppermute | solution.py:275
  30.8 2.7 %collective-permute-start.5 = (bf16[1024,512]{1,0:T(8,128)(2,1)S(1)}, bf16[1024,512]{1,0:T(8,128)(2,1)S(1)}, u32[]{:S(2)}, u32[]{:S(2)}) collective-permute-start(bf16[1024,512]{1,0:T(8,128)(2,1)S(1)} %collective-permute-done.4.near_ref), channel_id=1, source_target_pairs={{0,1},{1,0},{2,3},{3,2},{4,5},{5,4},{6,7},{7,6},{8,9},{9,8},{10,11... | collective-permute-start | bytes 3145736 | tf_op jit(solution)/shard_map/ppermute | solution.py:356
  36.9 6.5 %attend.1 = (bf16[512,512]{1,0:T(8,128)(2,1)}, bf16[512,512]{1,0:T(8,128)(2,1)}, bf16[512,512]{1,0:T(8,128)(2,1)}, bf16[512,512]{1,0:T(8,128)(2,1)}) custom-call(s32[6]{0:T(128)S(1)} %copy-done.8, s32[1]{0:T(128)} %bitcast.place_ref, bf16[512,512]{1,0:T(8,128)(2,1)S(1)} %copy-done.16, bf16[512,512]{1,0:T(8,128)(2,1)S(1)} %copy-done.18, ...), custom_call_target="tpu_custom_call" | custom-call | flops 1610612736 | bytes 4194304 | tf_op jit(solution)/shard_map/attend/pallas_call | solution.py:138
  44.9 3.3 %turn.3.own_ref = bf16[2048,512]{1,0:T(8,128)(2,1)S(1)} custom-call(s32[4]{0:T(128)S(1)} %multiply_add_fusion.list_ref, bf16[512,4096]{1,0:T(8,128)(2,1)} %x_ref.5), custom_call_target="tpu_custom_call" | custom-call | bytes 4194304 | tf_op jit(solution)/shard_map/turn/pallas_call | solution.py:160
  50.6 4.9 %collective-permute-done.22.h_ref = bf16[512,512]{1,0:T(8,128)(2,1)S(1)} collective-permute-done((bf16[512,512]{1,0:T(8,128)(2,1)}, bf16[512,512]{1,0:T(8,128)(2,1)S(1)}, u32[]{:S(2)}, u32[]{:S(2)}) %collective-permute-start.22) | collective-permute-done | bytes 524320 | tf_op jit(solution)/shard_map/ppermute | solution.py:366
  59.5 5.5 %share.5 = bf16[4,512,512]{2,1,0:T(8,128)(2,1)S(1)} custom-call(s32[4]{0:T(128)S(1)} %and_select_fusion.order_ref, bf16[2048,512]{1,0:T(8,128)(2,1)} %copy-done.7, bf16[1024,512]{1,0:T(8,128)(2,1)S(1)} %collective-permute-done.4.near_ref, bf16[1024,512]{1,0:T(8,128)(2,1)S(1)} %copy-done.10, bf16[512,512]{1,0:T(8,128)(2,1)} %get-tuple-element.33.v_ref.g_ref, ...), custom_call_target="tpu_custom_call" | custom-call | flops 2147483648 | bytes 7340032 | tf_op jit(solution)/shard_map/share/pallas_call | solution.py:198
  68.0 5.7 %share.4 = bf16[4,512,512]{2,1,0:T(8,128)(2,1)S(1)} custom-call(s32[4]{0:T(128)S(1)} %and_select_fusion.order_ref, bf16[2048,512]{1,0:T(8,128)(2,1)} %copy-done.7, bf16[1024,512]{1,0:T(8,128)(2,1)S(1)} %collective-permute-done.4.near_ref, bf16[1024,512]{1,0:T(8,128)(2,1)S(1)} %copy-done.11, bf16[512,512]{1,0:T(8,128)(2,1)} %get-tuple-element.32.k_ref.g_ref, ...), custom_call_target="tpu_custom_call" | custom-call | flops 2147483648 | bytes 7340032 | tf_op jit(solution)/shard_map/share/pallas_call | solution.py:198
  78.1 5.5 %share.3 = bf16[4,512,512]{2,1,0:T(8,128)(2,1)S(1)} custom-call(s32[4]{0:T(128)S(1)} %and_select_fusion.order_ref, bf16[2048,512]{1,0:T(8,128)(2,1)} %copy-done.7, bf16[1024,512]{1,0:T(8,128)(2,1)S(1)} %collective-permute-done.4.near_ref, bf16[1024,512]{1,0:T(8,128)(2,1)S(1)} %copy-done.11, bf16[512,512]{1,0:T(8,128)(2,1)} %get-tuple-element.31.g_ref.q_ref, ...), custom_call_target="tpu_custom_call" | custom-call | flops 2147483648 | bytes 7340032 | tf_op jit(solution)/shard_map/share/pallas_call | solution.py:198
  86.8 11.5 %inputs.1 = bf16[512,4096]{1,0:T(8,128)(2,1)S(1)} custom-call(bf16[512,512]{1,0:T(8,128)(2,1)} %get-tuple-element.31.g_ref.q_ref, bf16[512,512]{1,0:T(8,128)(2,1)} %get-tuple-element.32.k_ref.g_ref, bf16[512,512]{1,0:T(8,128)(2,1)} %get-tuple-element.33.v_ref.g_ref, bf16[4096,512]{1,0:T(8,128)(2,1)} %wq_ref.3, bf16[4096,512]{1,0:T(8,128)(2,1)} %wk_ref.3, ...), custom_call_target="tpu_custom_call" | custom-call | flops 6442450944 | bytes 16777216 | tf_op jit(solution)/shard_map/inputs/pallas_call | solution.py:233
  98.5 1.7 copy-done.5
  101.9 4.0 %collective-permute-start.7 = (bf16[256,4096]{1,0:T(8,128)(2,1)}, bf16[256,4096]{1,0:T(8,128)(2,1)}, u32[]{:S(2)}, u32[]{:S(2)}) collective-permute-start(bf16[256,4096]{1,0:T(8,128)(2,1)} %pad_maximum_fusion), channel_id=1, source_target_pairs={{0,1},{1,0},{2,3},{3,2},{4,5},{5,4},{6,7},{7,6},{8,9},{9,8},{10,11... | collective-permute-start | bytes 6291464 | tf_op jit(solution)/shard_map/ppermute | solution.py:323
  114.1 7.5 %collective-permute-done.24 = bf16[512,512]{1,0:T(8,128)(2,1)} collective-permute-done((bf16[512,512]{1,0:T(8,128)(2,1)S(1)}, bf16[512,512]{1,0:T(8,128)(2,1)}, u32[]{:S(2)}, u32[]{:S(2)}) %collective-permute-start.24) | collective-permute-done | bytes 524320 | tf_op jit(solution)/shard_map/ppermute | solution.py:303
  124.6 5.2 %collective-permute-start.27 = (bf16[512,512]{1,0:T(8,128)(2,1)S(1)}, bf16[512,512]{1,0:T(8,128)(2,1)S(1)}, u32[]{:S(2)}, u32[]{:S(2)}) collective-permute-start(bf16[512,512]{1,0:T(8,128)(2,1)S(1)} %get-tuple-element.42), channel_id=1, source_target_pairs={{16,8},{20,12},{24,16},{28,20},{17,9},{21,13},{25,17},{29,21},{18,... | collective-permute-start | bytes 1572872 | tf_op jit(solution)/shard_map/ppermute | solution.py:303
  129.7 3.0 %collective-permute-done.17 = bf16[512,512]{1,0:T(8,128)(2,1)S(1)} collective-permute-done((bf16[512,512]{1,0:T(8,128)(2,1)S(1)}, bf16[512,512]{1,0:T(8,128)(2,1)S(1)}, u32[]{:S(2)}, u32[]{:S(2)}) %collective-permute-start.17) | collective-permute-done | bytes 524320 | tf_op jit(solution)/shard_map/ppermute | solution.py:303
  132.7 1.9 collective-permute-start.25
  135.8 3.8 %collective-permute-start.20 = (bf16[512,512]{1,0:T(8,128)(2,1)S(1)}, bf16[512,512]{1,0:T(8,128)(2,1)S(1)}, u32[]{:S(2)}, u32[]{:S(2)}) collective-permute-start(bf16[512,512]{1,0:T(8,128)(2,1)S(1)} %get-tuple-element.46), channel_id=1, source_target_pairs={{16,8},{20,12},{24,16},{28,20},{17,9},{21,13},{25,17},{29,21},{18,... | collective-permute-start | bytes 1572872 | tf_op jit(solution)/shard_map/ppermute | solution.py:303
  139.6 4.4 %collective-permute-done.10 = bf16[512,512]{1,0:T(8,128)(2,1)S(1)} collective-permute-done((bf16[512,512]{1,0:T(8,128)(2,1)S(1)}, bf16[512,512]{1,0:T(8,128)(2,1)S(1)}, u32[]{:S(2)}, u32[]{:S(2)}) %collective-permute-start.10) | collective-permute-done | bytes 524320 | tf_op jit(solution)/shard_map/ppermute | solution.py:303
  143.9 1.9 collective-permute-start.18
  147.0 4.2 %collective-permute-start.13 = (bf16[512,512]{1,0:T(8,128)(2,1)S(1)}, bf16[512,512]{1,0:T(8,128)(2,1)S(1)}, u32[]{:S(2)}, u32[]{:S(2)}) collective-permute-start(bf16[512,512]{1,0:T(8,128)(2,1)S(1)} %get-tuple-element.50), channel_id=1, source_target_pairs={{16,8},{20,12},{24,16},{28,20},{17,9},{21,13},{25,17},{29,21},{18,... | collective-permute-start | bytes 1572872 | tf_op jit(solution)/shard_map/ppermute | solution.py:303
  151.4 6.9 %collective-permute-done.20 = bf16[512,512]{1,0:T(8,128)(2,1)S(1)} collective-permute-done((bf16[512,512]{1,0:T(8,128)(2,1)S(1)}, bf16[512,512]{1,0:T(8,128)(2,1)S(1)}, u32[]{:S(2)}, u32[]{:S(2)}) %collective-permute-start.20) | collective-permute-done | bytes 524320 | tf_op jit(solution)/shard_map/ppermute | solution.py:303
  158.3 1.9 collective-permute-start.28
  160.3 1.9 collective-permute-start.21
  163.8 5.7 %collective-permute-done.13 = bf16[512,512]{1,0:T(8,128)(2,1)S(1)} collective-permute-done((bf16[512,512]{1,0:T(8,128)(2,1)S(1)}, bf16[512,512]{1,0:T(8,128)(2,1)S(1)}, u32[]{:S(2)}, u32[]{:S(2)}) %collective-permute-start.13) | collective-permute-done | bytes 524320 | tf_op jit(solution)/shard_map/ppermute | solution.py:303
  170.9 1.9 collective-permute-start.11
  172.8 7.9 %collective-permute-done.28 = bf16[512,512]{1,0:T(8,128)(2,1)S(1)} collective-permute-done((bf16[512,512]{1,0:T(8,128)(2,1)S(1)}, bf16[512,512]{1,0:T(8,128)(2,1)S(1)}, u32[]{:S(2)}, u32[]{:S(2)}) %collective-permute-start.28) | collective-permute-done | bytes 524320 | tf_op jit(solution)/shard_map/ppermute | solution.py:303
  180.7 1.9 collective-permute-start.14
  183.8 8.1 %collective-permute-done.21 = bf16[512,512]{1,0:T(8,128)(2,1)S(1)} collective-permute-done((bf16[512,512]{1,0:T(8,128)(2,1)S(1)}, bf16[512,512]{1,0:T(8,128)(2,1)S(1)}, u32[]{:S(2)}, u32[]{:S(2)}) %collective-permute-start.21) | collective-permute-done | bytes 524320 | tf_op jit(solution)/shard_map/ppermute | solution.py:303
  193.1 10.1 %collective-permute-done.14 = bf16[512,512]{1,0:T(8,128)(2,1)S(1)} collective-permute-done((bf16[512,512]{1,0:T(8,128)(2,1)S(1)}, bf16[512,512]{1,0:T(8,128)(2,1)S(1)}, u32[]{:S(2)}, u32[]{:S(2)}) %collective-permute-start.14) | collective-permute-done | bytes 524320 | tf_op jit(solution)/shard_map/ppermute | solution.py:303
  204.4 2.7 %add_convert_fusion = bf16[128,4096]{1,0:T(8,128)(2,1)} fusion(bf16[128,4096]{1,0:T(8,128)(2,1)S(1)} %collective-permute-done.8, bf16[256,4096]{1,0:T(8,128)(2,1)} %collective-permute-done.7, bf16[512,4096]{1,0:T(8,128)(2,1)S(1)} %copy-done.6, s32[]{:T(128)S(6)} %select_n.82), kind=kLoop, calls=%fused_computation.1 | loop fusion | flops 4194304 | bytes 4194308 | tf_op jit(solution)/shard_map/convert_element_type | solution.py:329
  (103 shorter events, 50.4 us)
Async XLA Ops:
  3.9 26.8 %collective-permute-start.4 = (bf16[1024,512]{1,0:T(8,128)(2,1)S(1)}, bf16[1024,512]{1,0:T(8,128)(2,1)S(1)}, u32[]{:S(2)}, u32[]{:S(2)}) collective-permute-start(bf16[1024,512]{1,0:T(8,128)(2,1)S(1)} %turn.2), channel_id=1, source_target_pairs={{0,4},{4,0},{8,12},{12,8},{16,20},{20,16},{24,28},{28,24},{1,5},{5... | collective-permute-start | bytes 3145736 | tf_op jit(solution)/shard_map/ppermute | solution.py:355
  20.8 12.8 %collective-permute-start.2 = (bf16[4,128,128]{2,1,0:T(8,128)(2,1)S(1)}, bf16[4,128,128]{2,1,0:T(8,128)(2,1)S(1)}, u32[]{:S(2)}, u32[]{:S(2)}) collective-permute-start(bf16[4,128,128]{2,1,0:T(8,128)(2,1)S(1)} %get-tuple-element.25), channel_id=1, source_target_pairs={{4,0},{8,4},{12,8},{16,12},{20,16},{24,20},{28,24},{5,1},{9,5},{13... | collective-permute-start | bytes 393224 | tf_op jit(solution)/shard_map/ppermute | solution.py:278
  22.9 10.8 %collective-permute-start.3 = (bf16[4,128,128]{2,1,0:T(8,128)(2,1)S(1)}, bf16[4,128,128]{2,1,0:T(8,128)(2,1)S(1)}, u32[]{:S(2)}, u32[]{:S(2)}) collective-permute-start(bf16[4,128,128]{2,1,0:T(8,128)(2,1)S(1)} %get-tuple-element.25), channel_id=1, source_target_pairs={{8,0},{9,1},{10,2},{11,3}} | collective-permute-start | bytes 393224 | tf_op jit(solution)/shard_map/ppermute | solution.py:278
  23.6 10.1 %collective-permute-start = (bf16[4,128,128]{2,1,0:T(8,128)(2,1)S(1)}, bf16[4,128,128]{2,1,0:T(8,128)(2,1)S(1)}, u32[]{:S(2)}, u32[]{:S(2)}) collective-permute-start(bf16[4,128,128]{2,1,0:T(8,128)(2,1)S(1)} %get-tuple-element.24), channel_id=1, source_target_pairs={{0,4},{4,8},{8,12},{12,16},{16,20},{20,24},{24,28},{1,5},{5,9},{9,... | collective-permute-start | bytes 393224 | tf_op jit(solution)/shard_map/ppermute | solution.py:275
  26.8 6.9 %collective-permute-start.1 = (bf16[4,128,128]{2,1,0:T(8,128)(2,1)S(1)}, bf16[4,128,128]{2,1,0:T(8,128)(2,1)S(1)}, u32[]{:S(2)}, u32[]{:S(2)}) collective-permute-start(bf16[4,128,128]{2,1,0:T(8,128)(2,1)S(1)} %get-tuple-element.24), channel_id=1, source_target_pairs={{0,8},{1,9},{2,10},{3,11}} | collective-permute-start | bytes 393224 | tf_op jit(solution)/shard_map/ppermute | solution.py:275
  30.8 25.5 %collective-permute-start.5 = (bf16[1024,512]{1,0:T(8,128)(2,1)S(1)}, bf16[1024,512]{1,0:T(8,128)(2,1)S(1)}, u32[]{:S(2)}, u32[]{:S(2)}) collective-permute-start(bf16[1024,512]{1,0:T(8,128)(2,1)S(1)} %collective-permute-done.4.near_ref), channel_id=1, source_target_pairs={{0,1},{1,0},{2,3},{3,2},{4,5},{5,4},{6,7},{7,6},{8,9},{9,8},{10,11... | collective-permute-start | bytes 3145736 | tf_op jit(solution)/shard_map/ppermute | solution.py:356
  43.4 12.1 %collective-permute-start.22 = (bf16[512,512]{1,0:T(8,128)(2,1)}, bf16[512,512]{1,0:T(8,128)(2,1)S(1)}, u32[]{:S(2)}, u32[]{:S(2)}) collective-permute-start(bf16[512,512]{1,0:T(8,128)(2,1)} %get-tuple-element.33.v_ref.g_ref), channel_id=1, source_target_pairs={{0,4},{4,0},{8,12},{12,8},{16,20},{20,16},{24,28},{28,24},{1,5},{5... | collective-permute-start | bytes 1572872 | tf_op jit(solution)/shard_map/ppermute | solution.py:366
  44.5 23.4 %collective-permute-start.15 = (bf16[512,512]{1,0:T(8,128)(2,1)}, bf16[512,512]{1,0:T(8,128)(2,1)}, u32[]{:S(2)}, u32[]{:S(2)}) collective-permute-start(bf16[512,512]{1,0:T(8,128)(2,1)} %get-tuple-element.32.k_ref.g_ref), channel_id=1, source_target_pairs={{0,4},{4,0},{8,12},{12,8},{16,20},{20,16},{24,28},{28,24},{1,5},{5... | collective-permute-start | bytes 1572872 | tf_op jit(solution)/shard_map/ppermute | solution.py:366
  49.5 28.6 %collective-permute-start.6 = (bf16[512,512]{1,0:T(8,128)(2,1)}, bf16[512,512]{1,0:T(8,128)(2,1)S(1)}, u32[]{:S(2)}, u32[]{:S(2)}) collective-permute-start(bf16[512,512]{1,0:T(8,128)(2,1)} %get-tuple-element.31.g_ref.q_ref), channel_id=1, source_target_pairs={{0,4},{4,0},{8,12},{12,8},{16,20},{20,16},{24,28},{28,24},{1,5},{5... | collective-permute-start | bytes 1572872 | tf_op jit(solution)/shard_map/ppermute | solution.py:366
  66.0 39.9 %collective-permute-start.23 = (bf16[512,512]{1,0:T(8,128)(2,1)S(1)}, bf16[512,512]{1,0:T(8,128)(2,1)S(1)}, u32[]{:S(2)}, u32[]{:S(2)}) collective-permute-start(bf16[512,512]{1,0:T(8,128)(2,1)S(1)} %get-tuple-element.43), channel_id=1, source_target_pairs={{0,8},{4,12},{1,9},{5,13},{2,10},{6,14},{3,11},{7,15}} | collective-permute-start | bytes 1572872 | tf_op jit(solution)/shard_map/ppermute | solution.py:303
  66.7 46.1 %collective-permute-start.26 = (bf16[512,512]{1,0:T(8,128)(2,1)}, bf16[512,512]{1,0:T(8,128)(2,1)}, u32[]{:S(2)}, u32[]{:S(2)}) collective-permute-start(bf16[512,512]{1,0:T(8,128)(2,1)} %get-tuple-element.44), channel_id=1, source_target_pairs={{24,16},{28,20},{25,17},{29,21},{26,18},{30,22},{27,19},{31,23}} | collective-permute-start | bytes 1572872 | tf_op jit(solution)/shard_map/ppermute | solution.py:303
  76.1 31.3 %collective-permute-start.16 = (bf16[512,512]{1,0:T(8,128)(2,1)}, bf16[512,512]{1,0:T(8,128)(2,1)}, u32[]{:S(2)}, u32[]{:S(2)}) collective-permute-start(bf16[512,512]{1,0:T(8,128)(2,1)} %get-tuple-element.47), channel_id=1, source_target_pairs={{0,8},{4,12},{1,9},{5,13},{2,10},{6,14},{3,11},{7,15}} | collective-permute-start | bytes 1572872 | tf_op jit(solution)/shard_map/ppermute | solution.py:303
  86.1 24.1 %collective-permute-start.9 = (bf16[512,512]{1,0:T(8,128)(2,1)}, bf16[512,512]{1,0:T(8,128)(2,1)S(1)}, u32[]{:S(2)}, u32[]{:S(2)}) collective-permute-start(bf16[512,512]{1,0:T(8,128)(2,1)} %get-tuple-element.51), channel_id=1, source_target_pairs={{0,8},{4,12},{1,9},{5,13},{2,10},{6,14},{3,11},{7,15}} | collective-permute-start | bytes 1572872 | tf_op jit(solution)/shard_map/ppermute | solution.py:303
  101.9 58.5 %collective-permute-start.7 = (bf16[256,4096]{1,0:T(8,128)(2,1)}, bf16[256,4096]{1,0:T(8,128)(2,1)}, u32[]{:S(2)}, u32[]{:S(2)}) collective-permute-start(bf16[256,4096]{1,0:T(8,128)(2,1)} %pad_maximum_fusion), channel_id=1, source_target_pairs={{0,1},{1,0},{2,3},{3,2},{4,5},{5,4},{6,7},{7,6},{8,9},{9,8},{10,11... | collective-permute-start | bytes 6291464 | tf_op jit(solution)/shard_map/ppermute | solution.py:323
  106.0 15.6 %collective-permute-start.24 = (bf16[512,512]{1,0:T(8,128)(2,1)S(1)}, bf16[512,512]{1,0:T(8,128)(2,1)}, u32[]{:S(2)}, u32[]{:S(2)}) collective-permute-start(bf16[512,512]{1,0:T(8,128)(2,1)S(1)} %fusion.2), channel_id=1, source_target_pairs={{0,8},{4,12},{8,16},{12,20},{1,9},{5,13},{9,17},{13,21},{2,10},{6,... | collective-permute-start | bytes 1572872 | tf_op jit(solution)/shard_map/ppermute | solution.py:303
  107.4 17.2 %collective-permute-start.19 = (bf16[512,512]{1,0:T(8,128)(2,1)}, bf16[512,512]{1,0:T(8,128)(2,1)S(1)}, u32[]{:S(2)}, u32[]{:S(2)}) collective-permute-start(bf16[512,512]{1,0:T(8,128)(2,1)} %get-tuple-element.48), channel_id=1, source_target_pairs={{24,16},{28,20},{25,17},{29,21},{26,18},{30,22},{27,19},{31,23}} | collective-permute-start | bytes 1572872 | tf_op jit(solution)/shard_map/ppermute | solution.py:303
  110.1 24.5 %copy-start.2 = (bf16[4,512,512]{2,1,0:T(8,128)(2,1)S(1)}, bf16[4,512,512]{2,1,0:T(8,128)(2,1)}, u32[]{:S(2)}) copy-start(bf16[4,512,512]{2,1,0:T(8,128)(2,1)} %copy-done.1) | copy-start | bytes 6291460
  110.2 22.5 %collective-permute-start.17 = (bf16[512,512]{1,0:T(8,128)(2,1)S(1)}, bf16[512,512]{1,0:T(8,128)(2,1)S(1)}, u32[]{:S(2)}, u32[]{:S(2)}) collective-permute-start(bf16[512,512]{1,0:T(8,128)(2,1)S(1)} %fusion.7), channel_id=1, source_target_pairs={{0,8},{4,12},{8,16},{12,20},{1,9},{5,13},{9,17},{13,21},{2,10},{6,... | collective-permute-start | bytes 1572872 | tf_op jit(solution)/shard_map/ppermute | solution.py:303
  112.8 23.0 %collective-permute-start.12 = (bf16[512,512]{1,0:T(8,128)(2,1)S(1)}, bf16[512,512]{1,0:T(8,128)(2,1)S(1)}, u32[]{:S(2)}, u32[]{:S(2)}) collective-permute-start(bf16[512,512]{1,0:T(8,128)(2,1)S(1)} %copy-done.21), channel_id=1, source_target_pairs={{24,16},{28,20},{25,17},{29,21},{26,18},{30,22},{27,19},{31,23}} | collective-permute-start | bytes 1572872 | tf_op jit(solution)/shard_map/ppermute | solution.py:303
  121.6 22.4 %collective-permute-start.10 = (bf16[512,512]{1,0:T(8,128)(2,1)S(1)}, bf16[512,512]{1,0:T(8,128)(2,1)S(1)}, u32[]{:S(2)}, u32[]{:S(2)}) collective-permute-start(bf16[512,512]{1,0:T(8,128)(2,1)S(1)} %fusion.12), channel_id=1, source_target_pairs={{0,8},{4,12},{8,16},{12,20},{1,9},{5,13},{9,17},{13,21},{2,10},{6,... | collective-permute-start | bytes 1572872 | tf_op jit(solution)/shard_map/ppermute | solution.py:303
  124.4 21.5 %copy-start.4 = (bf16[4,512,512]{2,1,0:T(8,128)(2,1)S(1)}, bf16[4,512,512]{2,1,0:T(8,128)(2,1)}, u32[]{:S(2)}) copy-start(bf16[4,512,512]{2,1,0:T(8,128)(2,1)} %copy-done.3) | copy-start | bytes 6291460
  124.6 22.5 %collective-permute-start.27 = (bf16[512,512]{1,0:T(8,128)(2,1)S(1)}, bf16[512,512]{1,0:T(8,128)(2,1)S(1)}, u32[]{:S(2)}, u32[]{:S(2)}) collective-permute-start(bf16[512,512]{1,0:T(8,128)(2,1)S(1)} %get-tuple-element.42), channel_id=1, source_target_pairs={{16,8},{20,12},{24,16},{28,20},{17,9},{21,13},{25,17},{29,21},{18,... | collective-permute-start | bytes 1572872 | tf_op jit(solution)/shard_map/ppermute | solution.py:303
  132.7 38.2 %collective-permute-start.25 = (bf16[512,512]{1,0:T(8,128)(2,1)S(1)}, bf16[512,512]{1,0:T(8,128)(2,1)S(1)}, u32[]{:S(2)}, u32[]{:S(2)}) collective-permute-start(bf16[512,512]{1,0:T(8,128)(2,1)S(1)} %get-tuple-element.41), channel_id=1, source_target_pairs={{0,8},{4,12},{8,16},{12,20},{16,24},{20,28},{1,9},{5,13},{9,17},{1... | collective-permute-start | bytes 1572872 | tf_op jit(solution)/shard_map/ppermute | solution.py:303
  135.8 22.5 %collective-permute-start.20 = (bf16[512,512]{1,0:T(8,128)(2,1)S(1)}, bf16[512,512]{1,0:T(8,128)(2,1)S(1)}, u32[]{:S(2)}, u32[]{:S(2)}) collective-permute-start(bf16[512,512]{1,0:T(8,128)(2,1)S(1)} %get-tuple-element.46), channel_id=1, source_target_pairs={{16,8},{20,12},{24,16},{28,20},{17,9},{21,13},{25,17},{29,21},{18,... | collective-permute-start | bytes 1572872 | tf_op jit(solution)/shard_map/ppermute | solution.py:303
  143.9 39.9 %collective-permute-start.18 = (bf16[512,512]{1,0:T(8,128)(2,1)S(1)}, bf16[512,512]{1,0:T(8,128)(2,1)S(1)}, u32[]{:S(2)}, u32[]{:S(2)}) collective-permute-start(bf16[512,512]{1,0:T(8,128)(2,1)S(1)} %get-tuple-element.45), channel_id=1, source_target_pairs={{0,8},{4,12},{8,16},{12,20},{16,24},{20,28},{1,9},{5,13},{9,17},{1... | collective-permute-start | bytes 1572872 | tf_op jit(solution)/shard_map/ppermute | solution.py:303
  145.9 16.4 %copy-start.6 = (bf16[512,4096]{1,0:T(8,128)(2,1)S(1)}, bf16[512,4096]{1,0:T(8,128)(2,1)}, u32[]{:S(2)}) copy-start(bf16[512,4096]{1,0:T(8,128)(2,1)} %copy-done.5) | copy-start | bytes 12582916
  147.0 22.5 %collective-permute-start.13 = (bf16[512,512]{1,0:T(8,128)(2,1)S(1)}, bf16[512,512]{1,0:T(8,128)(2,1)S(1)}, u32[]{:S(2)}, u32[]{:S(2)}) collective-permute-start(bf16[512,512]{1,0:T(8,128)(2,1)S(1)} %get-tuple-element.50), channel_id=1, source_target_pairs={{16,8},{20,12},{24,16},{28,20},{17,9},{21,13},{25,17},{29,21},{18,... | collective-permute-start | bytes 1572872 | tf_op jit(solution)/shard_map/ppermute | solution.py:303
  158.3 22.5 %collective-permute-start.28 = (bf16[512,512]{1,0:T(8,128)(2,1)S(1)}, bf16[512,512]{1,0:T(8,128)(2,1)S(1)}, u32[]{:S(2)}, u32[]{:S(2)}) collective-permute-start(bf16[512,512]{1,0:T(8,128)(2,1)S(1)} %fusion.1), channel_id=1, source_target_pairs={{8,0},{12,4},{16,8},{20,12},{24,16},{28,20},{9,1},{13,5},{17,9},{2... | collective-permute-start | bytes 1572872 | tf_op jit(solution)/shard_map/ppermute | solution.py:303
  160.3 31.6 %collective-permute-start.21 = (bf16[512,512]{1,0:T(8,128)(2,1)S(1)}, bf16[512,512]{1,0:T(8,128)(2,1)S(1)}, u32[]{:S(2)}, u32[]{:S(2)}) collective-permute-start(bf16[512,512]{1,0:T(8,128)(2,1)S(1)} %fusion.6), channel_id=1, source_target_pairs={{8,0},{12,4},{16,8},{20,12},{24,16},{28,20},{9,1},{13,5},{17,9},{2... | collective-permute-start | bytes 1572872 | tf_op jit(solution)/shard_map/ppermute | solution.py:303
  169.5 34.9 %collective-permute-start.8 = (bf16[128,4096]{1,0:T(8,128)(2,1)S(1)}, bf16[128,4096]{1,0:T(8,128)(2,1)S(1)}, u32[]{:S(2)}, u32[]{:S(2)}) collective-permute-start(bf16[128,4096]{1,0:T(8,128)(2,1)S(1)} %add_convert_fusion.1), channel_id=1, source_target_pairs={{0,2},{1,3},{2,0},{3,1},{4,6},{5,7},{6,4},{7,5},{8,10},{9,11},{10,... | collective-permute-start | bytes 3145736 | tf_op jit(solution)/shard_map/ppermute | solution.py:323
  170.9 22.2 %collective-permute-start.11 = (bf16[512,512]{1,0:T(8,128)(2,1)S(1)}, bf16[512,512]{1,0:T(8,128)(2,1)S(1)}, u32[]{:S(2)}, u32[]{:S(2)}) collective-permute-start(bf16[512,512]{1,0:T(8,128)(2,1)S(1)} %get-tuple-element.49), channel_id=1, source_target_pairs={{0,8},{4,12},{8,16},{12,20},{16,24},{20,28},{1,9},{5,13},{9,17},{1... | collective-permute-start | bytes 1572872 | tf_op jit(solution)/shard_map/ppermute | solution.py:303
  180.7 22.5 %collective-permute-start.14 = (bf16[512,512]{1,0:T(8,128)(2,1)S(1)}, bf16[512,512]{1,0:T(8,128)(2,1)S(1)}, u32[]{:S(2)}, u32[]{:S(2)}) collective-permute-start(bf16[512,512]{1,0:T(8,128)(2,1)S(1)} %fusion.11), channel_id=1, source_target_pairs={{8,0},{12,4},{16,8},{20,12},{24,16},{28,20},{9,1},{13,5},{17,9},{2... | collective-permute-start | bytes 1572872 | tf_op jit(solution)/shard_map/ppermute | solution.py:303
  (19 other events, 30.8 us)
where the time goes:
time: 208 us; the launch traced here: 207 us
  waiting for transfers between devices  61 us (29%)
  starting transfers between devices  54 us (26%)
  Pallas kernels  52.3 us (25%)
  local copies, waits for them, and re-layouts  20.7 us (10%)
  other arithmetic  15.4 us (7%)
  between operations  3.77 us (2%)
    ppermute x18, waiting for transfers between devices, line_scatter(): carried = lax.ppermute(sent, 'seq', pairs)  55.4 us
    ppermute x18, starting transfers between devices, line_scatter(): carried = lax.ppermute(sent, 'seq', pairs)  35.5 us
    unnamed x44, local copies, waits for them, and re-layouts  17.5 us
    pallas_call x3, Pallas kernels, share(): pl.pallas_call(functools.partial(share_kernel, half, scale), grid_spec=pl...  16.7 us
    pallas_call x1, Pallas kernels, project(): pl.pallas_call(functools.partial(project_kernel, starts.shape[0]), grid_s...  13.2 us
    pallas_call x1, Pallas kernels, inputs(): pl.pallas_call(inputs_kernel, grid=(width // piece,), in_specs=[pl.BlockS...  11.5 us
    pallas_call x1, Pallas kernels, attend(): pl.pallas_call(functools.partial(attend_kernel, starts.shape[0]), grid_sp...  6.5 us
    ppermute x3, waiting for transfers between devices, on_device(): got = [lax.ppermute(grad, 'seq', swap) for grad in rows]  5.4 us
  transfers between devices with their start and end apart: 29, of which 14 were waited for; matrix products, arithmetic and copies ran while one was open for 8% of the time, Pallas kernels for 25%

commit v1 on v0

--- a/solution.py
+++ b/solution.py
@@ -13,7 +13,7 @@
 
 
 def params():
-    return pltpu.CompilerParams(vmem_limit_bytes=48 * 1024 * 1024)
+    return pltpu.CompilerParams(vmem_limit_bytes=58 * 1024 * 1024)
 
 
 def cost(flops, bytes_accessed):
@@ -172,52 +172,6 @@
     )(blocks, tokens)
 
 
-def share_kernel(half, scale, order_ref, own_ref, near_ref, far_ref, g_ref, h_ref, o_ref):
-    step = pl.program_id(0)
-    total = jnp.dot(own_ref[...], g_ref[...], preferred_element_type=F32)
-
-    def write(got):
-        both = total + jnp.dot(got, h_ref[...], preferred_element_type=F32)
-        o_ref[0] = (scale * both).astype(LOW)
-
-    @pl.when(step < half)
-    def _():
-        write(near_ref[...])
-
-    @pl.when(step >= half)
-    def _():
-        write(far_ref[...])
-
-
-def share(order, own, near, far, grad_own, grad_got, scale):
-    length = order.shape[0]
-    piece = own.shape[0] // length
-    rows, cols = grad_own.shape
-    half = near.shape[0] // piece
-    grad = pl.BlockSpec((rows, cols), lambda i, at: (0, 0))
-    return pl.pallas_call(
-        functools.partial(share_kernel, half, scale),
-        grid_spec=pltpu.PrefetchScalarGridSpec(
-            num_scalar_prefetch=1,
-            grid=(length,),
-            in_specs=[
-                pl.BlockSpec((piece, rows), lambda i, at: (at[i], 0)),
-                pl.BlockSpec((piece, rows), lambda i, at: (jnp.minimum(i, half - 1), 0)),
-                pl.BlockSpec((piece, rows), lambda i, at: (jnp.maximum(i - half, 0), 0)),
-                grad,
-                grad,
-            ],
-            out_specs=pl.BlockSpec((1, piece, cols), lambda i, at: (at[i], 0, 0)),
-        ),
-        out_shape=jax.ShapeDtypeStruct((length, piece, cols), LOW),
-        compiler_params=params(),
-        cost_estimate=cost(
-            4 * length * piece * rows * cols, 2 * (3 * length * piece * rows + 2 * rows * cols)
-        ),
-        name="share",
-    )(order, own, near, far, grad_own, grad_got)
-
-
 def inputs_kernel(q_ref, k_ref, v_ref, wq_ref, wk_ref, wv_ref, o_ref):
     last = ((1,), (1,))
     total = dot(q_ref[...], wq_ref[...], last)
@@ -281,56 +235,191 @@
     return state_in.astype(jnp.bfloat16), reverse_in.astype(jnp.bfloat16)
 
 
-def line_scatter(parts):
-    span_total = lax.axis_size("seq")
-    length = span_total // 2
-    place = lax.axis_index("seq") // 2
-
-    def part_for(target):
-        return lax.dynamic_index_in_dim(parts, jnp.clip(target, 0, length - 1), 0, keepdims=False)
-
-    total = part_for(place).astype(jnp.float32)
-    for way in (1, -1):
-        carried = None
-        for step in range(1, length):
-            ahead = way * (length - step)
-            sent = part_for(place + ahead)
-            if carried is not None:
-                sent = (sent.astype(jnp.float32) + carried.astype(jnp.float32)).astype(jnp.bfloat16)
-            pairs = [
-                (s, s + 2 * way) for s in range(span_total) if 0 <= s // 2 + ahead < length
-            ]
-            carried = lax.ppermute(sent, "seq", pairs)
-        if carried is not None:
-            total = total + carried.astype(jnp.float32)
-    return total
-
-
-def halving_scatter(partial):
-    count = lax.axis_size("mp")
-    index = lax.axis_index("mp")
-    size = partial.shape[0] // count
-
-    def pick(k):
-        return lax.dynamic_slice_in_dim(partial, jnp.bitwise_xor(index, k) * size, size, 0)
-
-    held = {k: pick(k) for k in range(count)}
+def flip(index, bit):
+    return index + bit - 2 * bit * ((index // bit) % 2)
+
+
+def finish_kernel(
+    length, members, scale, own_ref, near_ref, far_ref, gq_ref, gk_ref, gv_ref, hq_ref, part_ref,
+    oq_ref, ok_ref, ov_ref, oi_ref, shares, swapped, carried, bits,
+    swap_send, swap_recv, line_send, line_recv, bit_send, bit_recv,
+):
+    spot, member = lax.axis_index("seq"), lax.axis_index("mp")
+    total = 2 * length
+    place = spot // 2
+    half = length // 2
+    shift = half * (member % 2)
+    piece = own_ref.shape[0] // length
+    size = part_ref.shape[0] // members
+    grads = (gq_ref, gk_ref, gv_ref)
+    outs = (oq_ref, ok_ref, ov_ref)
+
+    barrier = pltpu.get_barrier_semaphore()
+    friends = [
+        {"seq": flip(spot, 1)},
+        {"seq": (spot + 2) % total},
+        {"seq": (spot + total - 2) % total},
+    ]
+    turns = []
     bit = 1
-    while bit < count:
-        pairs = [(m, m ^ bit) for m in range(count)]
-        away = [k for k in held if k & bit]
-        sent = jnp.concatenate([held[k] for k in away], axis=0) if len(away) > 1 else held[away[0]]
-        got = lax.ppermute(sent, "mp", pairs)
-        kind = jnp.bfloat16
-        held = {
-            k ^ bit: (
-                held[k ^ bit].astype(jnp.float32)
-                + got[i * size : (i + 1) * size].astype(jnp.float32)
-            ).astype(kind)
-            for i, k in enumerate(away)
-        }
+    while bit < members:
+        friends.append({"mp": flip(member, bit)})
+        turns.append(bit)
         bit *= 2
-    return held[0]
+    for friend in friends:
+        pl.semaphore_signal(barrier, inc=1, device_id=friend, device_id_type=pl.DeviceIdType.MESH)
+    pl.semaphore_wait(barrier, len(friends))
+
+    def remote(src, dst, send, recv, where):
+        return pltpu.make_async_remote_copy(
+            src_ref=src, dst_ref=dst, send_sem=send, recv_sem=recv,
+            device_id=where, device_id_type=pl.DeviceIdType.MESH,
+        )
+
+    def swap(j):
+        return remote(
+            grads[j], swapped.at[j - 1], swap_send.at[j - 1], swap_recv.at[j - 1],
+            {"seq": flip(spot, 1)},
+        )
+
+    def other(k):
+        at = member
+        for bit in turns:
+            if k & bit:
+                at = flip(at, bit)
+        return pl.ds(pl.multiple_of(at * size, size), size)
+
+    rounds = [[k for k in range(1, members) if k % (2 * b) == b] for b in turns]
+
+    def held(r, k):
+        return part_ref.at[other(k)] if r == 0 else bits.at[k + turns[r - 1] - 1]
+
+    def bit_copy(r, k):
+        return remote(
+            held(r, k), bits.at[k - 1], bit_send.at[k - 1], bit_recv.at[k - 1],
+            {"mp": flip(member, turns[r])},
+        )
+
+    def bit_start(r):
+        for k in rounds[r]:
+            bit_copy(r, k).start()
+
+    def bit_end(r):
+        for k in rounds[r]:
+            bit_copy(r, k).wait()
+            both = held(r, k - turns[r])[...].astype(F32) + bits[k - 1].astype(F32)
+            bits[k - 1] = both.astype(LOW)
+
+    def share(j):
+        mine = grads[j]
+        theirs = hq_ref if j == 0 else swapped.at[j - 1]
+        for first, got_ref in ((0, near_ref), (half, far_ref)):
+
+            def body(i, _):
+                z = (i + first + shift) % length
+                rows = pl.ds(pl.multiple_of(z * piece, piece), piece)
+                got = got_ref[pl.ds(pl.multiple_of(i * piece, piece), piece), :]
+                term = jnp.dot(own_ref[rows, :], mine[...], preferred_element_type=F32)
+                term = term + jnp.dot(got, theirs[...], preferred_element_type=F32)
+                shares[j, z] = (scale * term).astype(LOW)
+                return 0
+
+            lax.fori_loop(0, half, body, 0)
+
+    rank = (place, length - 1 - place)
+
+    def line(step, j, way, first):
+        target = place + (length - step if way == 0 else step - length)
+        near_by = (spot + (2 if way == 0 else total - 2)) % total
+        src = shares.at[j, (target + length) % length] if first else carried.at[way, step - 2, j]
+        return remote(
+            src, carried.at[way, step - 1, j],
+            line_send.at[way, step - 1, j], line_recv.at[way, step - 1, j], {"seq": near_by},
+        )
+
+    def send(step, j):
+        for way in (0, 1):
+
+            @pl.when(rank[way] == 0)
+            def _():
+                line(step, j, way, True).start()
+
+            if step > 1:
+
+                @pl.when((rank[way] >= 1) & (rank[way] <= step - 1))
+                def _():
+                    line(step - 1, j, way, True).wait_recv()
+                    target = (place + length + (length - step if way == 0 else step - length)) % length
+                    both = carried[way, step - 2, j].astype(F32) + shares[j, target].astype(F32)
+                    carried[way, step - 2, j] = both.astype(LOW)
+                    line(step, j, way, False).start()
+
+    swap(1).start()
+    share(0)
+    send(1, 0)
+    bit_start(0)
+    swap(1).wait()
+    swap(2).start()
+    share(1)
+    send(1, 1)
+    bit_end(0)
+    bit_start(1)
+    swap(2).wait()
+    share(2)
+    send(1, 2)
+    for step in range(2, length):
+        for j in range(3):
+            send(step, j)
+    bit_end(1)
+    oi_ref[...] = bits[turns[1] - 1]
+    for j in range(3):
+        outs[j][...] = shares[j, place].astype(F32)
+        for way in (0, 1):
+
+            @pl.when(rank[way] >= 1)
+            def _():
+                line(length - 1, j, way, True).wait_recv()
+                outs[j][...] += carried[way, length - 2, j].astype(F32)
+
+    for step in range(1, length):
+        for j in range(3):
+            for way in (0, 1):
+
+                @pl.when(rank[way] <= step - 1)
+                def _():
+                    line(step, j, way, True).wait_send()
+
+
+def finish(own, near, far, grads, first_got, partial, scale):
+    length = lax.axis_size("seq") // 2
+    members = lax.axis_size("mp")
+    piece = own.shape[0] // length
+    rows, cols = grads[0].shape
+    size, width = partial.shape[0] // members, partial.shape[1]
+    vmem = pl.BlockSpec(memory_space=pltpu.VMEM)
+    dma = pltpu.SemaphoreType.DMA
+    *sums, input_grad = pl.pallas_call(
+        functools.partial(finish_kernel, length, members, scale),
+        in_specs=[vmem] * 8,
+        out_specs=[vmem] * 4,
+        out_shape=[jax.ShapeDtypeStruct((piece, cols), F32)] * 3
+        + [jax.ShapeDtypeStruct((size, width), LOW)],
+        scratch_shapes=[
+            pltpu.VMEM((3, length, piece, cols), LOW),
+            pltpu.VMEM((2, rows, cols), LOW),
+            pltpu.VMEM((2, length - 1, 3, piece, cols), LOW),
+            pltpu.VMEM((members - 1, size, width), LOW),
+            dma((2,)), dma((2,)),
+            dma((2, length - 1, 3)), dma((2, length - 1, 3)),
+            dma((members - 1,)), dma((members - 1,)),
+        ],
+        compiler_params=pltpu.CompilerParams(
+            collective_id=0, has_side_effects=True, vmem_limit_bytes=58 * 1024 * 1024
+        ),
+        cost_estimate=cost(12 * length * piece * rows * cols, 16 * 1024 * 1024),
+        name="finish",
+    )(own, near, far, *grads, first_got, partial)
+    return sums, input_grad
 
 
 def on_device(tokens, w_query, w_key, w_value, starts, cotangent):
@@ -360,16 +449,13 @@
     )
     own = turn(2 * turn_order + side, tokens, piece)
     state_in, reverse_in = linked_states(forward_part, backward_part, starts, row_count)
+    begin, own = lax.optimization_barrier((begin, own))
     attended, *rows = attend(
         starts, begin, queries, keys, values, cotangent, state_in, reverse_in
     )
-    got = [lax.ppermute(grad, "seq", swap) for grad in rows]
-    shares = [
-        share(order, own, near, far, mine, theirs, grad_scale) for mine, theirs in zip(rows, got)
-    ]
-    rows, shares[0] = lax.optimization_barrier((rows, shares[0]))
-    sums = [line_scatter(parts) for parts in shares]
-    input_grad = halving_scatter(inputs(rows, weights))
+    first_got = lax.ppermute(rows[0], "seq", swap)
+    partial = inputs(rows, weights)
+    sums, input_grad = finish(own, near, far, rows, first_got, partial, grad_scale)
     return (attended, input_grad, *sums)
 
 

time: 208 us -> 186 us (0.89)
  Pallas kernels: 52.3 us -> 157 us
  waiting for transfers between devices: 61 us -> 0.55 us
  starting transfers between devices: 54 us -> 10.5 us
  local copies, waits for them, and re-layouts: 20.7 us -> 8.41 us
  other arithmetic: 15.4 us -> 3.16 us
    pallas_call x3 -> x1, Pallas kernels: 16.7 us -> 114 us  [finish(): pl.pallas_call(functools.partial(finish_kernel, length, members, scale),...]
    ppermute x23 -> x1, waiting for transfers between devices: 60.8 us -> 0.54 us  [on_device(): first_got = lax.ppermute(rows[0], 'seq', swap)]
    ppermute x23 -> x1, starting transfers between devices: 43.3 us -> 0.05 us  [on_device(): first_got = lax.ppermute(rows[0], 'seq', swap)]
    convert_element_type x11 -> x0, other arithmetic: 9.37 us -> none  [the longest x9 5.21 us: line_scatter(): (sent.astype(jnp.float32) + carried.astype(jnp.float32)).astype(jnp.bfloa...]
    unnamed x44 -> x16, local copies, waits for them, and re-layouts: 17.5 us -> 8.41 us
    add x3 -> x0, other arithmetic: 3.51 us -> none  [line_scatter(): total = total + carried.astype(jnp.float32)]
    pallas_call x2, Pallas kernels: 4.32 us -> 7.67 us  [turn(): pl.pallas_call(turn_kernel, grid_spec=pltpu.PrefetchScalarGridSpec(num_sc...]
    squeeze x3 -> x0, local copies, waits for them, and re-layouts: 3 us -> none  [part_for(): lax.dynamic_index_in_dim(parts, jnp.clip(target, 0, length - 1), 0, keepd...]
  transfers between devices with their start and end apart: 29 -> 7, of which waited for: 14 -> 1; matrix products, arithmetic and copies ran while one was open for 8% -> 1% of each run, Pallas kernels for 25% -> 22%
where the time goes in v1:
time: 186 us; the launch traced here: 183 us
  Pallas kernels  157 us (84%)
  starting transfers between devices  10.5 us (6%)
  local copies, waits for them, and re-layouts  8.41 us (5%)
  between operations  3.21 us (2%)
  other arithmetic  3.16 us (2%)
    pallas_call x1, Pallas kernels, finish(): pl.pallas_call(functools.partial(finish_kernel, length, members, scale),...  114 us
    pallas_call x1, Pallas kernels, project(): pl.pallas_call(functools.partial(project_kernel, starts.shape[0]), grid_s...  15.5 us
    pallas_call x1, Pallas kernels, inputs(): pl.pallas_call(inputs_kernel, grid=(width // piece,), in_specs=[pl.BlockS...  13 us
    unnamed x16, local copies, waits for them, and re-layouts  8.41 us
    pallas_call x2, Pallas kernels, turn(): pl.pallas_call(turn_kernel, grid_spec=pltpu.PrefetchScalarGridSpec(num_sc...  7.67 us
    pallas_call x1, Pallas kernels, attend(): pl.pallas_call(functools.partial(attend_kernel, starts.shape[0]), grid_sp...  7.34 us
    ppermute x2, starting transfers between devices, linked_states(): lax.ppermute(backward_part, 'seq', [(high, low) for low, high in pairs])  4.69 us
  transfers between devices with their start and end apart: 7, of which 1 were waited for; matrix products, arithmetic and copies ran while one was open for 1% of the time, Pallas kernels for 22%

profile of v1, /device:TPU:17, one launch (start us, length us, event | category | flops | bytes accessed | tf_op | source)
XLA Modules:
  0.0 183.0 jit_solution(9992227272236345977)
XLA Ops:
  0.7 0.5 add_subtract_fusion.list_ref
  1.2 2.9 %turn.2 = bf16[1024,512]{1,0:T(8,128)(2,1)} custom-call(s32[2]{0:T(128)} %add_subtract_fusion.list_ref, bf16[512,4096]{1,0:T(8,128)(2,1)} %x_ref.5), custom_call_target="tpu_custom_call" | custom-call | bytes 2097152 | tf_op jit(solution)/shard_map/turn/pallas_call | solution.py:160
  4.1 1.2 collective-permute-start.4
  5.3 15.5 %project.1 = (bf16[512,512]{1,0:T(8,128)(2,1)}, bf16[512,512]{1,0:T(8,128)(2,1)}, bf16[512,512]{1,0:T(8,128)(2,1)}, bf16[4,128,128]{2,1,0:T(8,128)(2,1)}, bf16[4,128,128]{2,1,0:T(8,128)(2,1)}) custom-call(s32[6]{0:T(128)} %starts_ref.3, s32[1]{0:T(128)} %bitcast.place_ref, bf16[512,4096]{1,0:T(8,128)(2,1)} %x_ref.5, bf16[4096,512]{1,0:T(8,128)(2,1)} %wq_ref.3, ...), custom_call_target="tpu_custom_call" | custom-call | flops 6442450944 | bytes 16777216 | tf_op jit(solution)/shard_map/project/pallas_call | solution.py:89
  20.8 0.8 collective-permute-start.1
  21.6 2.2 %collective-permute-start = (bf16[4,128,128]{2,1,0:T(8,128)(2,1)}, bf16[4,128,128]{2,1,0:T(8,128)(2,1)S(1)}, u32[]{:S(2)}, u32[]{:S(2)}) collective-permute-start(bf16[4,128,128]{2,1,0:T(8,128)(2,1)} %get-tuple-element.27), channel_id=1, source_target_pairs={{0,4},{4,8},{8,12},{12,16},{16,20},{20,24},{24,28},{1,5},{5,9},{9,... | collective-permute-start | bytes 393224 | tf_op jit(solution)/shard_map/ppermute | solution.py:229
  23.8 0.7 collective-permute-start.3
  24.4 4.0 %collective-permute-start.2 = (bf16[4,128,128]{2,1,0:T(8,128)(2,1)}, bf16[4,128,128]{2,1,0:T(8,128)(2,1)S(1)}, u32[]{:S(2)}, u32[]{:S(2)}) collective-permute-start(bf16[4,128,128]{2,1,0:T(8,128)(2,1)} %get-tuple-element.28), channel_id=1, source_target_pairs={{4,0},{8,4},{12,8},{16,12},{20,16},{24,20},{28,24},{5,1},{9,5},{13... | collective-permute-start | bytes 393224 | tf_op jit(solution)/shard_map/ppermute | solution.py:232
  28.5 0.5 multiply_add_fusion.list_ref
  29.0 4.8 %turn.3.own_ref = bf16[2048,512]{1,0:T(8,128)(2,1)} custom-call(s32[4]{0:T(128)} %multiply_add_fusion.list_ref, bf16[512,4096]{1,0:T(8,128)(2,1)} %x_ref.5), custom_call_target="tpu_custom_call" | custom-call | bytes 4194304 | tf_op jit(solution)/shard_map/turn/pallas_call | solution.py:160
  33.8 0.7 fusion.3
  36.9 0.0 collective-permute-done.4.near_ref
  36.9 0.0 copy-start.3
  37.0 1.6 collective-permute-start.5
  38.5 0.0 collective-permute-done.1
  38.5 0.0 collective-permute-done
  38.5 0.7 add_convert_fusion.1.s_ref
  39.2 0.0 collective-permute-done.3
  39.2 0.0 collective-permute-done.2
  39.2 0.7 add_convert_fusion.r_ref
  39.9 7.3 %attend.1 = (bf16[512,512]{1,0:T(8,128)(2,1)}, bf16[512,512]{1,0:T(8,128)(2,1)}, bf16[512,512]{1,0:T(8,128)(2,1)}, bf16[512,512]{1,0:T(8,128)(2,1)}) custom-call(s32[6]{0:T(128)} %starts_ref.3, s32[1]{0:T(128)} %bitcast.place_ref, bf16[512,512]{1,0:T(8,128)(2,1)} %get-tuple-element.24.q_ref, bf16[512,512]{1,0:T(8,128)(2,1)} %get-tuple-element.25.k_ref, ...), custom_call_target="tpu_custom_call" | custom-call | flops 1610612736 | bytes 4194304 | tf_op jit(solution)/shard_map/attend/pallas_call | solution.py:138
  47.3 0.0 collective-permute-start.6
  47.3 13.0 %inputs.1.part_ref = bf16[512,4096]{1,0:T(8,128)(2,1)} custom-call(bf16[512,512]{1,0:T(8,128)(2,1)} %get-tuple-element.32.q_ref.gq_ref, bf16[512,512]{1,0:T(8,128)(2,1)} %get-tuple-element.33.k_ref.gk_ref, bf16[512,512]{1,0:T(8,128)(2,1)} %get-tuple-element.34.v_ref.gv_ref, bf16[4096,512]{1,0:T(8,128)(2,1)} %wq_ref.3, bf16[4096,512]{1,0:T(8,128)(2,1)} %wk_ref.3, ...), custom_call_target="tpu_custom_call" | custom-call | flops 6442450944 | bytes 16777216 | tf_op jit(solution)/shard_map/inputs/pallas_call | solution.py:187
  60.3 0.5 collective-permute-done.6.hq_ref
  60.9 0.0 collective-permute-done.5.far_ref
  60.9 0.8 copy-done.5
  61.7 1.0 copy-done.4
  62.6 113.7 %finish.1 = (f32[512,512]{1,0:T(8,128)}, f32[512,512]{1,0:T(8,128)}, f32[512,512]{1,0:T(8,128)}, bf16[128,4096]{1,0:T(8,128)(2,1)}) custom-call(bf16[2048,512]{1,0:T(8,128)(2,1)} %turn.3.own_ref, bf16[1024,512]{1,0:T(8,128)(2,1)} %copy-done.3, bf16[1024,512]{1,0:T(8,128)(2,1)} %copy-done.4, bf16[512,512]{1,0:T(8,128)(2,1)} %get-tuple-element.32.q_ref.gq_ref, ...), custom_call_target="tpu_custom_call" | custom-call | flops 6442450944 | bytes 16777216 | tf_op jit(solution)/shard_map/finish/pallas_call | solution.py:401
  176.4 2.4 %copy.15 = bf16[128,4096]{1,0:T(8,128)(2,1)} copy(bf16[128,4096]{1,0:T(8,128)(2,1)} %get-tuple-element.49) | data formatting | bytes 2097152
  178.8 2.3 %copy.16 = f32[512,512]{1,0:T(8,128)} copy(f32[512,512]{1,0:T(8,128)} %get-tuple-element.50) | data formatting | bytes 2097152
  181.1 1.0 copy.17
  182.0 1.0 copy.18
  (10 shorter events, 0.0 us)
Async XLA Ops:
  4.1 32.8 %collective-permute-start.4 = (bf16[1024,512]{1,0:T(8,128)(2,1)}, bf16[1024,512]{1,0:T(8,128)(2,1)S(1)}, u32[]{:S(2)}, u32[]{:S(2)}) collective-permute-start(bf16[1024,512]{1,0:T(8,128)(2,1)} %turn.2), channel_id=1, source_target_pairs={{0,4},{4,0},{8,12},{12,8},{16,20},{20,16},{24,28},{28,24},{1,5},{5... | collective-permute-start | bytes 3145736 | tf_op jit(solution)/shard_map/ppermute | solution.py:444
  20.8 13.0 %copy-start.2 = (s32[6]{0:T(128)S(1)}, s32[6]{0:T(128)}, u32[]{:S(2)}) copy-start(s32[6]{0:T(128)} %starts_ref.3) | copy-start | bytes 76
  20.8 17.7 %collective-permute-start.1 = (bf16[4,128,128]{2,1,0:T(8,128)(2,1)}, bf16[4,128,128]{2,1,0:T(8,128)(2,1)S(1)}, u32[]{:S(2)}, u32[]{:S(2)}) collective-permute-start(bf16[4,128,128]{2,1,0:T(8,128)(2,1)} %get-tuple-element.27), channel_id=1, source_target_pairs={{0,8},{1,9},{2,10},{3,11}} | collective-permute-start | bytes 393224 | tf_op jit(solution)/shard_map/ppermute | solution.py:229
  21.6 16.9 %collective-permute-start = (bf16[4,128,128]{2,1,0:T(8,128)(2,1)}, bf16[4,128,128]{2,1,0:T(8,128)(2,1)S(1)}, u32[]{:S(2)}, u32[]{:S(2)}) collective-permute-start(bf16[4,128,128]{2,1,0:T(8,128)(2,1)} %get-tuple-element.27), channel_id=1, source_target_pairs={{0,4},{4,8},{8,12},{12,16},{16,20},{20,24},{24,28},{1,5},{5,9},{9,... | collective-permute-start | bytes 393224 | tf_op jit(solution)/shard_map/ppermute | solution.py:229
  23.8 15.5 %collective-permute-start.3 = (bf16[4,128,128]{2,1,0:T(8,128)(2,1)}, bf16[4,128,128]{2,1,0:T(8,128)(2,1)S(1)}, u32[]{:S(2)}, u32[]{:S(2)}) collective-permute-start(bf16[4,128,128]{2,1,0:T(8,128)(2,1)} %get-tuple-element.28), channel_id=1, source_target_pairs={{8,0},{9,1},{10,2},{11,3}} | collective-permute-start | bytes 393224 | tf_op jit(solution)/shard_map/ppermute | solution.py:232
  24.4 14.8 %collective-permute-start.2 = (bf16[4,128,128]{2,1,0:T(8,128)(2,1)}, bf16[4,128,128]{2,1,0:T(8,128)(2,1)S(1)}, u32[]{:S(2)}, u32[]{:S(2)}) collective-permute-start(bf16[4,128,128]{2,1,0:T(8,128)(2,1)} %get-tuple-element.28), channel_id=1, source_target_pairs={{4,0},{8,4},{12,8},{16,12},{20,16},{24,20},{28,24},{5,1},{9,5},{13... | collective-permute-start | bytes 393224 | tf_op jit(solution)/shard_map/ppermute | solution.py:232
  36.9 23.4 %copy-start.3 = (bf16[1024,512]{1,0:T(8,128)(2,1)}, bf16[1024,512]{1,0:T(8,128)(2,1)S(1)}, u32[]{:S(2)}) copy-start(bf16[1024,512]{1,0:T(8,128)(2,1)S(1)} %collective-permute-done.4.near_ref) | copy-start | bytes 3145732
  37.0 23.9 %collective-permute-start.5 = (bf16[1024,512]{1,0:T(8,128)(2,1)S(1)}, bf16[1024,512]{1,0:T(8,128)(2,1)S(1)}, u32[]{:S(2)}, u32[]{:S(2)}) collective-permute-start(bf16[1024,512]{1,0:T(8,128)(2,1)S(1)} %collective-permute-done.4.near_ref), channel_id=1, source_target_pairs={{0,1},{1,0},{2,3},{3,2},{4,5},{5,4},{6,7},{7,6},{8,9},{9,8},{10,11... | collective-permute-start | bytes 3145736 | tf_op jit(solution)/shard_map/ppermute | solution.py:445
  47.3 13.6 %collective-permute-start.6 = (bf16[512,512]{1,0:T(8,128)(2,1)}, bf16[512,512]{1,0:T(8,128)(2,1)S(1)}, u32[]{:S(2)}, u32[]{:S(2)}) collective-permute-start(bf16[512,512]{1,0:T(8,128)(2,1)} %get-tuple-element.32.q_ref.gq_ref), channel_id=1, source_target_pairs={{0,4},{4,0},{8,12},{12,8},{16,20},{20,16},{24,28},{28,24},{1,5},{5... | collective-permute-start | bytes 1572872 | tf_op jit(solution)/shard_map/ppermute | solution.py:456
  60.9 0.8 copy-start.5
  61.7 1.0 copy-start.4
  176.3 4.7 %copy-start.1 = (f32[512,512]{1,0:T(8,128)S(1)}, f32[512,512]{1,0:T(8,128)}, u32[]{:S(2)}) copy-start(f32[512,512]{1,0:T(8,128)} %get-tuple-element.51) | copy-start | bytes 3145732
  176.4 5.7 %copy-start = (f32[512,512]{1,0:T(8,128)S(1)}, f32[512,512]{1,0:T(8,128)}, u32[]{:S(2)}) copy-start(f32[512,512]{1,0:T(8,128)} %get-tuple-element.52) | copy-start | bytes 3145732

commit v2 on v1

--- a/solution.py
+++ b/solution.py
@@ -172,31 +172,6 @@
     )(blocks, tokens)
 
 
-def inputs_kernel(q_ref, k_ref, v_ref, wq_ref, wk_ref, wv_ref, o_ref):
-    last = ((1,), (1,))
-    total = dot(q_ref[...], wq_ref[...], last)
-    total = total + dot(k_ref[...], wk_ref[...], last)
-    total = total + dot(v_ref[...], wv_ref[...], last)
-    o_ref[...] = total.astype(LOW)
-
-
-def inputs(grads, weights):
-    rows, cols = grads[0].shape
-    width = weights[0].shape[0]
-    piece = min(512, width)
-    return pl.pallas_call(
-        inputs_kernel,
-        grid=(width // piece,),
-        in_specs=[pl.BlockSpec((rows, cols), lambda i: (0, 0))] * 3
-        + [pl.BlockSpec((piece, cols), lambda i: (i, 0))] * 3,
-        out_specs=pl.BlockSpec((rows, piece), lambda i: (0, i)),
-        out_shape=jax.ShapeDtypeStruct((rows, width), LOW),
-        compiler_params=params(),
-        cost_estimate=cost(6 * rows * width * cols, 2 * (rows * width + 3 * width * cols)),
-        name="inputs",
-    )(*grads, *weights)
-
-
 def linked_pairs(token_count, span_total, start_count):
     first = token_count // 4
     stratum = (token_count - first) // start_count
@@ -240,9 +215,9 @@
 
 
 def finish_kernel(
-    length, members, scale, own_ref, near_ref, far_ref, gq_ref, gk_ref, gv_ref, hq_ref, part_ref,
-    oq_ref, ok_ref, ov_ref, oi_ref, shares, swapped, carried, bits,
-    swap_send, swap_recv, line_send, line_recv, bit_send, bit_recv,
+    length, members, scale, own_hbm, near_hbm, far_hbm, gq_ref, gk_ref, gv_ref, wq_hbm, wk_hbm,
+    wv_hbm, oq_ref, ok_ref, ov_ref, oi_ref, own_ref, near_ref, far_ref, wide, part_ref, shares,
+    swapped, carried, bits, load_sem, swap_send, swap_recv, line_send, line_recv, bit_send, bit_recv,
 ):
     spot, member = lax.axis_index("seq"), lax.axis_index("mp")
     total = 2 * length
@@ -253,6 +228,22 @@
     size = part_ref.shape[0] // members
     grads = (gq_ref, gk_ref, gv_ref)
     outs = (oq_ref, ok_ref, ov_ref)
+
+    loads = [
+        pltpu.make_async_copy(src, dst, load_sem.at[i])
+        for i, (src, dst) in enumerate(
+            [
+                (wq_hbm, wide.at[0]),
+                (wk_hbm, wide.at[1]),
+                (wv_hbm, wide.at[2]),
+                (own_hbm, own_ref),
+                (near_hbm, near_ref),
+                (far_hbm, far_ref),
+            ]
+        )
+    ]
+    for load in loads:
+        load.start()
 
     barrier = pltpu.get_barrier_semaphore()
     friends = [
@@ -278,7 +269,7 @@
 
     def swap(j):
         return remote(
-            grads[j], swapped.at[j - 1], swap_send.at[j - 1], swap_recv.at[j - 1],
+            grads[j], swapped.at[j], swap_send.at[j], swap_recv.at[j],
             {"seq": flip(spot, 1)},
         )
 
@@ -312,7 +303,7 @@
 
     def share(j):
         mine = grads[j]
-        theirs = hq_ref if j == 0 else swapped.at[j - 1]
+        theirs = swapped.at[j]
         for first, got_ref in ((0, near_ref), (half, far_ref)):
 
             def body(i, _):
@@ -354,6 +345,24 @@
                     carried[way, step - 2, j] = both.astype(LOW)
                     line(step, j, way, False).start()
 
+    swap(0).start()
+    for load in loads[:3]:
+        load.wait()
+    width = wide.shape[1]
+    strip = min(512, width)
+
+    def strips(i, _):
+        at = pl.ds(pl.multiple_of(i * strip, strip), strip)
+        term = dot(gq_ref[...], wide[0, at, :], ((1,), (1,)))
+        term = term + dot(gk_ref[...], wide[1, at, :], ((1,), (1,)))
+        term = term + dot(gv_ref[...], wide[2, at, :], ((1,), (1,)))
+        part_ref[:, at] = term.astype(LOW)
+        return 0
+
+    lax.fori_loop(0, width // strip, strips, 0)
+    for load in loads[3:]:
+        load.wait()
+    swap(0).wait()
     swap(1).start()
     share(0)
     send(1, 0)
@@ -390,26 +399,33 @@
                     line(step, j, way, True).wait_send()
 
 
-def finish(own, near, far, grads, first_got, partial, scale):
+def finish(own, near, far, grads, weights, scale):
     length = lax.axis_size("seq") // 2
     members = lax.axis_size("mp")
     piece = own.shape[0] // length
     rows, cols = grads[0].shape
-    size, width = partial.shape[0] // members, partial.shape[1]
+    size, width = rows // members, weights[0].shape[0]
     vmem = pl.BlockSpec(memory_space=pltpu.VMEM)
+    hbm = pl.BlockSpec(memory_space=pl.ANY)
     dma = pltpu.SemaphoreType.DMA
     *sums, input_grad = pl.pallas_call(
         functools.partial(finish_kernel, length, members, scale),
-        in_specs=[vmem] * 8,
+        in_specs=[hbm] * 3 + [vmem] * 3 + [hbm] * 3,
         out_specs=[vmem] * 4,
         out_shape=[jax.ShapeDtypeStruct((piece, cols), F32)] * 3
         + [jax.ShapeDtypeStruct((size, width), LOW)],
         scratch_shapes=[
+            pltpu.VMEM(own.shape, LOW),
+            pltpu.VMEM(near.shape, LOW),
+            pltpu.VMEM(far.shape, LOW),
+            pltpu.VMEM((3, width, cols), LOW),
+            pltpu.VMEM((rows, width), LOW),
             pltpu.VMEM((3, length, piece, cols), LOW),
-            pltpu.VMEM((2, rows, cols), LOW),
+            pltpu.VMEM((3, rows, cols), LOW),
             pltpu.VMEM((2, length - 1, 3, piece, cols), LOW),
             pltpu.VMEM((members - 1, size, width), LOW),
-            dma((2,)), dma((2,)),
+            dma((6,)),
+            dma((3,)), dma((3,)),
             dma((2, length - 1, 3)), dma((2, length - 1, 3)),
             dma((members - 1,)), dma((members - 1,)),
         ],
@@ -418,7 +434,7 @@
         ),
         cost_estimate=cost(12 * length * piece * rows * cols, 16 * 1024 * 1024),
         name="finish",
-    )(own, near, far, *grads, first_got, partial)
+    )(own, near, far, *grads, *weights)
     return sums, input_grad
 
 
@@ -453,9 +469,7 @@
     attended, *rows = attend(
         starts, begin, queries, keys, values, cotangent, state_in, reverse_in
     )
-    first_got = lax.ppermute(rows[0], "seq", swap)
-    partial = inputs(rows, weights)
-    sums, input_grad = finish(own, near, far, rows, first_got, partial, grad_scale)
+    sums, input_grad = finish(own, near, far, rows, weights, grad_scale)
     return (attended, input_grad, *sums)
 
 

time: 186 us -> 204 us (1.097)
  waiting for transfers between devices: 0.55 us -> 23 us
  Pallas kernels: 157 us -> 152 us
    ppermute x1, waiting for transfers between devices: 0.01 us -> 23 us  [on_device(): near = lax.ppermute(away, 'seq', swap)]
    pallas_call x1 -> x0, Pallas kernels: 13 us -> none  [inputs(): pl.pallas_call(inputs_kernel, grid=(width // piece,), in_specs=[pl.BlockS...]
    pallas_call x1, Pallas kernels: 114 us -> 122 us  [finish(): pl.pallas_call(functools.partial(finish_kernel, length, members, scale),...]
    unnamed x16 -> x14, local copies, waits for them, and re-layouts: 8.41 us -> 7.62 us
  transfers between devices with their start and end apart: 7 -> 6, of which waited for: 1 -> 1; matrix products, arithmetic and copies ran while one was open for 1% -> 1% of each run, Pallas kernels for 22% -> 14%
where the time goes in v2:
time: 204 us; the launch traced here: 200 us
  Pallas kernels  152 us (75%)
  waiting for transfers between devices  23 us (11%)
  starting transfers between devices  10.3 us (5%)
  local copies, waits for them, and re-layouts  7.62 us (4%)
  between operations  3.22 us (2%)
  other arithmetic  3.2 us (2%)
    pallas_call x1, Pallas kernels, finish(): pl.pallas_call(functools.partial(finish_kernel, length, members, scale),...  122 us
    ppermute x1, waiting for transfers between devices, on_device(): near = lax.ppermute(away, 'seq', swap)  23 us
    pallas_call x1, Pallas kernels, project(): pl.pallas_call(functools.partial(project_kernel, starts.shape[0]), grid_s...  15.5 us
    pallas_call x2, Pallas kernels, turn(): pl.pallas_call(turn_kernel, grid_spec=pltpu.PrefetchScalarGridSpec(num_sc...  7.66 us
    unnamed x14, local copies, waits for them, and re-layouts  7.62 us
    pallas_call x1, Pallas kernels, attend(): pl.pallas_call(functools.partial(attend_kernel, starts.shape[0]), grid_sp...  7.34 us
  transfers between devices with their start and end apart: 6, of which 1 were waited for; matrix products, arithmetic and copies ran while one was open for 1% of the time, Pallas kernels for 14%

profile of v2, /device:TPU:17, one launch (start us, length us, event | category | flops | bytes accessed | tf_op | source)
XLA Modules:
  0.0 199.7 jit_solution(9845566542044098468)
XLA Ops:
  0.7 0.5 add_subtract_fusion.list_ref
  1.2 2.9 %turn.2 = bf16[1024,512]{1,0:T(8,128)(2,1)} custom-call(s32[2]{0:T(128)} %add_subtract_fusion.list_ref, bf16[512,4096]{1,0:T(8,128)(2,1)} %x_ref.5), custom_call_target="tpu_custom_call" | custom-call | bytes 2097152 | tf_op jit(solution)/shard_map/turn/pallas_call | solution.py:160
  4.1 1.2 collective-permute-start.4
  5.3 23.0 %collective-permute-done.4.near_hbm = bf16[1024,512]{1,0:T(8,128)(2,1)S(1)} collective-permute-done((bf16[1024,512]{1,0:T(8,128)(2,1)}, bf16[1024,512]{1,0:T(8,128)(2,1)S(1)}, u32[]{:S(2)}, u32[]{:S(2)}) %collective-permute-start.4) | collective-permute-done | bytes 1048608 | tf_op jit(solution)/shard_map/ppermute | solution.py:460
  28.3 1.5 collective-permute-start.5
  29.9 15.5 %project.1 = (bf16[512,512]{1,0:T(8,128)(2,1)}, bf16[512,512]{1,0:T(8,128)(2,1)}, bf16[512,512]{1,0:T(8,128)(2,1)}, bf16[4,128,128]{2,1,0:T(8,128)(2,1)}, bf16[4,128,128]{2,1,0:T(8,128)(2,1)}) custom-call(s32[6]{0:T(128)} %starts_ref.3, s32[1]{0:T(128)} %bitcast.place_ref, bf16[512,4096]{1,0:T(8,128)(2,1)} %x_ref.5, bf16[4096,512]{1,0:T(8,128)(2,1)} %wq_hbm.1, ...), custom_call_target="tpu_custom_call" | custom-call | flops 6442450944 | bytes 16777216 | tf_op jit(solution)/shard_map/project/pallas_call | solution.py:89
  45.4 0.0 copy-done.3
  45.4 0.7 collective-permute-start.1
  46.1 3.1 %collective-permute-start = (bf16[4,128,128]{2,1,0:T(8,128)(2,1)}, bf16[4,128,128]{2,1,0:T(8,128)(2,1)S(1)}, u32[]{:S(2)}, u32[]{:S(2)}) collective-permute-start(bf16[4,128,128]{2,1,0:T(8,128)(2,1)} %get-tuple-element.27), channel_id=1, source_target_pairs={{0,4},{4,8},{8,12},{12,16},{16,20},{20,24},{24,28},{1,5},{5,9},{9,... | collective-permute-start | bytes 393224 | tf_op jit(solution)/shard_map/ppermute | solution.py:204
  49.2 0.7 collective-permute-start.3
  49.9 3.1 %collective-permute-start.2 = (bf16[4,128,128]{2,1,0:T(8,128)(2,1)}, bf16[4,128,128]{2,1,0:T(8,128)(2,1)S(1)}, u32[]{:S(2)}, u32[]{:S(2)}) collective-permute-start(bf16[4,128,128]{2,1,0:T(8,128)(2,1)} %get-tuple-element.28), channel_id=1, source_target_pairs={{4,0},{8,4},{12,8},{16,12},{20,16},{24,20},{28,24},{5,1},{9,5},{13... | collective-permute-start | bytes 393224 | tf_op jit(solution)/shard_map/ppermute | solution.py:207
  53.0 0.6 multiply_add_fusion.list_ref
  53.5 4.7 %turn.3.own_hbm = bf16[2048,512]{1,0:T(8,128)(2,1)} custom-call(s32[4]{0:T(128)} %multiply_add_fusion.list_ref, bf16[512,4096]{1,0:T(8,128)(2,1)} %x_ref.5), custom_call_target="tpu_custom_call" | custom-call | bytes 4194304 | tf_op jit(solution)/shard_map/turn/pallas_call | solution.py:160
  58.3 0.0 copy-done.2
  58.3 0.7 fusion.3
  61.5 0.0 collective-permute-done.1
  61.5 0.0 collective-permute-done
  61.5 0.7 add_convert_fusion.1.s_ref
  62.2 0.0 collective-permute-done.3
  62.2 0.0 collective-permute-done.2
  62.2 0.7 add_convert_fusion.r_ref
  62.9 7.3 %attend.1 = (bf16[512,512]{1,0:T(8,128)(2,1)}, bf16[512,512]{1,0:T(8,128)(2,1)}, bf16[512,512]{1,0:T(8,128)(2,1)}, bf16[512,512]{1,0:T(8,128)(2,1)}) custom-call(s32[6]{0:T(128)} %starts_ref.3, s32[1]{0:T(128)} %bitcast.place_ref, bf16[512,512]{1,0:T(8,128)(2,1)} %get-tuple-element.24.q_ref, bf16[512,512]{1,0:T(8,128)(2,1)} %get-tuple-element.25.k_ref, ...), custom_call_target="tpu_custom_call" | custom-call | flops 1610612736 | bytes 4194304 | tf_op jit(solution)/shard_map/attend/pallas_call | solution.py:138
  70.2 0.0 collective-permute-done.5.far_hbm
  70.2 0.0 copy-start.4
  70.2 1.0 copy-done.4
  71.2 121.8 %finish.1 = (f32[512,512]{1,0:T(8,128)}, f32[512,512]{1,0:T(8,128)}, f32[512,512]{1,0:T(8,128)}, bf16[128,4096]{1,0:T(8,128)(2,1)}) custom-call(bf16[2048,512]{1,0:T(8,128)(2,1)} %turn.3.own_hbm, bf16[1024,512]{1,0:T(8,128)(2,1)} %copy-done.3, bf16[1024,512]{1,0:T(8,128)(2,1)} %copy-done.4, bf16[512,512]{1,0:T(8,128)(2,1)} %get-tuple-element.32.gq_ref, ...), custom_call_target="tpu_custom_call" | custom-call | flops 6442450944 | bytes 16777216 | tf_op jit(solution)/shard_map/finish/pallas_call | solution.py:411
  193.1 0.0 copy-start.1
  193.1 0.0 copy-start
  193.1 2.4 %copy.15 = bf16[128,4096]{1,0:T(8,128)(2,1)} copy(bf16[128,4096]{1,0:T(8,128)(2,1)} %get-tuple-element.49) | data formatting | bytes 2097152
  195.5 2.3 %copy.16 = f32[512,512]{1,0:T(8,128)} copy(f32[512,512]{1,0:T(8,128)} %get-tuple-element.50) | data formatting | bytes 2097152
  197.8 1.0 copy.17
  198.8 1.0 copy.18
  (5 shorter events, 0.0 us)
Async XLA Ops:
  4.1 24.2 %collective-permute-start.4 = (bf16[1024,512]{1,0:T(8,128)(2,1)}, bf16[1024,512]{1,0:T(8,128)(2,1)S(1)}, u32[]{:S(2)}, u32[]{:S(2)}) collective-permute-start(bf16[1024,512]{1,0:T(8,128)(2,1)} %turn.2), channel_id=1, source_target_pairs={{0,4},{4,0},{8,12},{12,8},{16,20},{20,16},{24,28},{28,24},{1,5},{5... | collective-permute-start | bytes 3145736 | tf_op jit(solution)/shard_map/ppermute | solution.py:460
  28.3 17.1 %copy-start.3 = (bf16[1024,512]{1,0:T(8,128)(2,1)}, bf16[1024,512]{1,0:T(8,128)(2,1)S(1)}, u32[]{:S(2)}) copy-start(bf16[1024,512]{1,0:T(8,128)(2,1)S(1)} %collective-permute-done.4.near_hbm) | copy-start | bytes 3145732
  28.3 41.9 %collective-permute-start.5 = (bf16[1024,512]{1,0:T(8,128)(2,1)S(1)}, bf16[1024,512]{1,0:T(8,128)(2,1)S(1)}, u32[]{:S(2)}, u32[]{:S(2)}) collective-permute-start(bf16[1024,512]{1,0:T(8,128)(2,1)S(1)} %collective-permute-done.4.near_hbm), channel_id=1, source_target_pairs={{0,1},{1,0},{2,3},{3,2},{4,5},{5,4},{6,7},{7,6},{8,9},{9,8},{10,11... | collective-permute-start | bytes 3145736 | tf_op jit(solution)/shard_map/ppermute | solution.py:461
  45.4 12.9 %copy-start.2 = (s32[6]{0:T(128)S(1)}, s32[6]{0:T(128)}, u32[]{:S(2)}) copy-start(s32[6]{0:T(128)} %starts_ref.3) | copy-start | bytes 76
  45.4 16.1 %collective-permute-start.1 = (bf16[4,128,128]{2,1,0:T(8,128)(2,1)}, bf16[4,128,128]{2,1,0:T(8,128)(2,1)S(1)}, u32[]{:S(2)}, u32[]{:S(2)}) collective-permute-start(bf16[4,128,128]{2,1,0:T(8,128)(2,1)} %get-tuple-element.27), channel_id=1, source_target_pairs={{0,8},{1,9},{2,10},{3,11}} | collective-permute-start | bytes 393224 | tf_op jit(solution)/shard_map/ppermute | solution.py:204
  46.1 15.4 %collective-permute-start = (bf16[4,128,128]{2,1,0:T(8,128)(2,1)}, bf16[4,128,128]{2,1,0:T(8,128)(2,1)S(1)}, u32[]{:S(2)}, u32[]{:S(2)}) collective-permute-start(bf16[4,128,128]{2,1,0:T(8,128)(2,1)} %get-tuple-element.27), channel_id=1, source_target_pairs={{0,4},{4,8},{8,12},{12,16},{16,20},{20,24},{24,28},{1,5},{5,9},{9,... | collective-permute-start | bytes 393224 | tf_op jit(solution)/shard_map/ppermute | solution.py:204
  49.2 13.0 %collective-permute-start.3 = (bf16[4,128,128]{2,1,0:T(8,128)(2,1)}, bf16[4,128,128]{2,1,0:T(8,128)(2,1)S(1)}, u32[]{:S(2)}, u32[]{:S(2)}) collective-permute-start(bf16[4,128,128]{2,1,0:T(8,128)(2,1)} %get-tuple-element.28), channel_id=1, source_target_pairs={{8,0},{9,1},{10,2},{11,3}} | collective-permute-start | bytes 393224 | tf_op jit(solution)/shard_map/ppermute | solution.py:207
  49.9 12.3 %collective-permute-start.2 = (bf16[4,128,128]{2,1,0:T(8,128)(2,1)}, bf16[4,128,128]{2,1,0:T(8,128)(2,1)S(1)}, u32[]{:S(2)}, u32[]{:S(2)}) collective-permute-start(bf16[4,128,128]{2,1,0:T(8,128)(2,1)} %get-tuple-element.28), channel_id=1, source_target_pairs={{4,0},{8,4},{12,8},{16,12},{20,16},{24,20},{28,24},{5,1},{9,5},{13... | collective-permute-start | bytes 393224 | tf_op jit(solution)/shard_map/ppermute | solution.py:207
  70.2 1.0 copy-start.4
  193.1 4.7 %copy-start.1 = (f32[512,512]{1,0:T(8,128)S(1)}, f32[512,512]{1,0:T(8,128)}, u32[]{:S(2)}) copy-start(f32[512,512]{1,0:T(8,128)} %get-tuple-element.51) | copy-start | bytes 3145732
  193.1 5.7 %copy-start = (f32[512,512]{1,0:T(8,128)S(1)}, f32[512,512]{1,0:T(8,128)}, u32[]{:S(2)}) copy-start(f32[512,512]{1,0:T(8,128)} %get-tuple-element.52) | copy-start | bytes 3145732
